TPU v7x, 512 devices: a whole 4x4x16 slice. The times are simulated.
512 devices in a mesh: dp: 128 (over z, x, y_lo), sub: 4 (over y_hi, core).
Axes of the slice: x: 4, y: 4 (y_hi: 2, y_lo: 2; y = y_hi * 2 + y_lo), z: 16, core: 2. Of those that a mesh axis runs over, the one named last changes fastest.
Arguments:
- queries: bfloat16 [16384, 4096], P('dp', 'sub'), may hold values from -1 to 1
- passages: bfloat16 [768, 4096], P('dp', 'sub'), may hold values from -1 to 1
- positive_bank: bfloat16 [2048, 4096], P('dp', 'sub'), may hold values from -1 to 1
- positive_ids: int32 [16384, 16], P('dp'), may hold values from -1 to 2047, as said below
- positive_counts: int32 [16384], P('dp'), may hold values from 1 to 16
Outputs:
- losses: float32 [16384], P('dp')
- query_grad: float32 [16384, 4096], P('dp', 'sub')
- passage_grad: float32 [768, 4096], P('dp', 'sub')
- bank_grad: float32 [2048, 4096], P('dp', 'sub')
Inputs may be any that keep to these rules, and one draw needn't show every extreme that they name: `positive_ids`: entries of row i before position positive_counts[i] are rows of positive_bank, the rest are -1. The valid entries of the 128 queries of one index of dp name rows held by any one index of dp at most 2 times in all (repeats counted), a bound that is reached. In each aligned block of 16 queries at most one query has more than one valid entry.
All inputs are finite; a program needn't handle non-finite values.
Results may differ from a plain program's by a relative error of at most 0.0019.
Values may be sent and summed in bfloat16 or wider, within the bound.
A program may use at most 64 MiB of HBM per device.

v0:
```python
import jax
import jax.numpy as jnp
from jax import lax
from jax.sharding import PartitionSpec as P


def softmax_terms(score_sums, pos_sums, counts):
    scores = score_sums * 50.0
    pos_scores = pos_sums * 50.0
    is_valid = jnp.arange(pos_scores.shape[1])[None, :] < counts[:, None]
    row_max = jnp.maximum(jnp.max(scores, 1), jnp.max(jnp.where(is_valid, pos_scores, -jnp.inf), 1))
    row_total = jnp.sum(jnp.exp(scores - row_max[:, None]), 1)
    row_total = row_total + jnp.sum(
        jnp.exp(jnp.where(is_valid, pos_scores - row_max[:, None], -jnp.inf)), 1
    )
    log_total = row_max + jnp.log(row_total)
    inv_count = 1.0 / counts.astype(jnp.float32)
    query_loss = log_total - jnp.sum(jnp.where(is_valid, pos_scores, 0.0), 1) * inv_count
    weights = jnp.exp(scores - log_total[:, None]).astype(jnp.bfloat16)
    coeffs = jnp.where(
        is_valid,
        jnp.exp(jnp.where(is_valid, pos_scores - log_total[:, None], -jnp.inf))
        - inv_count[:, None],
        0.0,
    )
    return (query_loss, weights, coeffs)


def body(queries, passages, positive_bank, positive_ids, positive_counts):
    peer_count = lax.axis_size("dp")
    query_count, col_width = queries.shape
    bank_rows = positive_bank.shape[0]
    capacity = bank_rows // 8
    max_pos = positive_ids.shape[1]
    slot_total = peer_count * capacity
    flat_ids = positive_ids.reshape(-1)
    is_live = (jnp.arange(max_pos)[None, :] < positive_counts[:, None]).reshape(-1)
    owner_dev = jnp.where(is_live, flat_ids // bank_rows, 0)
    onehot = ((owner_dev[:, None] == jnp.arange(peer_count)[None, :]) & is_live[:, None]).astype(
        jnp.int32
    )
    slot_rank = jnp.sum(jnp.cumsum(onehot, 0) * onehot, 1) - 1
    slot_of = jnp.where(is_live, owner_dev * capacity + slot_rank, slot_total)
    local_ids = jnp.where(is_live, flat_ids % bank_rows, -1)
    send_ids = jnp.full((slot_total + 1,), -1, jnp.int32).at[slot_of].set(local_ids)[:slot_total]
    slot_request = (
        jnp.zeros((slot_total + 1,), jnp.int32)
        .at[slot_of]
        .set(jnp.arange(flat_ids.shape[0], dtype=jnp.int32))[:slot_total]
    )
    slot_live = send_ids >= 0
    slot_query = slot_request // max_pos
    wanted = lax.all_to_all(
        send_ids.reshape(peer_count, capacity), "dp", split_axis=0, concat_axis=0, tiled=True
    ).reshape(-1)
    served = wanted >= 0
    picked = jnp.where(
        served[:, None],
        positive_bank[jnp.clip(wanted, 0, bank_rows - 1)],
        jnp.zeros((), jnp.bfloat16),
    )
    fetched = lax.all_to_all(
        picked.reshape(peer_count, capacity, col_width),
        "dp",
        split_axis=0,
        concat_axis=0,
        tiled=True,
    ).reshape(slot_total, col_width)
    query_slots = queries[slot_query]
    slot_scores = jnp.einsum("sd,sd->s", query_slots, fetched, preferred_element_type=jnp.float32)
    pos_part = jnp.concatenate([slot_scores, jnp.zeros((1,), jnp.float32)])[slot_of].reshape(
        query_count, max_pos
    )
    all_passages = lax.all_gather(passages, "dp", axis=0, tiled=True)
    score_part = lax.dot_general(
        queries, all_passages, (((1,), (1,)), ((), ())), preferred_element_type=jnp.float32
    )
    score_sums, pos_sums = lax.psum((score_part, pos_part), "sub")
    losses, weights, coeffs = softmax_terms(score_sums, pos_sums, positive_counts)
    slot_coeff = jnp.where(slot_live, coeffs.reshape(-1)[slot_request], 0.0)
    pos_grad = jax.ops.segment_sum(
        slot_coeff[:, None] * fetched.astype(jnp.float32), slot_query, query_count
    )
    query_grad = 50.0 * (
        jnp.dot(weights, all_passages, preferred_element_type=jnp.float32) + pos_grad
    )
    passage_grad = 50.0 * lax.psum_scatter(
        lax.dot_general(
            weights, queries, (((0,), (0,)), ((), ())), preferred_element_type=jnp.float32
        ),
        "dp",
        scatter_dimension=0,
        tiled=True,
    )
    grad_rows = (slot_coeff[:, None] * query_slots.astype(jnp.float32)).reshape(
        peer_count, capacity, col_width
    )
    bank_terms = lax.all_to_all(grad_rows, "dp", split_axis=0, concat_axis=0, tiled=True).reshape(
        slot_total, col_width
    )
    member = (
        jnp.where(served, wanted, bank_rows)[None, :] == jnp.arange(bank_rows)[:, None]
    ).astype(jnp.float32)
    bank_grad = 50.0 * jnp.dot(member, bank_terms, precision=lax.Precision.HIGHEST)
    return (losses, query_grad, passage_grad, bank_grad)


def solution(mesh):
    placed = (P("dp", "sub"), P("dp", "sub"), P("dp", "sub"), P("dp", None), P("dp"))
    return jax.shard_map(
        body,
        mesh=mesh,
        in_specs=placed,
        out_specs=(P("dp"), P("dp", "sub"), P("dp", "sub"), P("dp", "sub")),
        check_vma=False,
    )
```

profile of v0, /device:TPU:4, one launch (start us, length us, event | category | flops | bytes accessed | tf_op | source)
XLA Modules:
  0.0 1185.8 jit_solution(14348177609646131720)
XLA Ops:
  13.5 8.0 scatter_custom_fusion.1
  21.7 34.1 %all_to_all.19 = s32[128,1,2]{2,1,0:T(1,128)S(1)} all-to-all(s32[128,1,2]{2,1,0:T(1,128)S(1)} %bitcast.24), channel_id=1, replica_groups=mesh['dp'=128,'sub'=4] {'dp'}, dimensions={0} | all-to-all | bytes 2048 | tf_op jit(solution)/shard_map/all_to_all | solution.py:53
  59.3 1.4 broadcast_select_fusion
  60.6 7.0 all-to-all-start.1
  67.6 8.2 scatter_custom_fusion
  77.6 1.7 reshape.304
  79.3 20.0 %all-to-all-done.1 = bf16[128,2,1024]{2,1,0:T(2,128)(2,1)S(1)} async-done(((bf16[128,2,1024]{2,1,0:T(2,128)(2,1)}), bf16[128,2,1024]{2,1,0:T(2,128)(2,1)S(1)}, u32[]{:S(2)}, u32[]{:S(2)}) %all-to-all-start.1) | async-done | bytes 524320 | tf_op jit(solution)/shard_map/all_to_all | solution.py:62
  99.5 499.5 %all-gather.3.cloned.1.call-done = bf16[128,6,1024]{2,1,0:T(8,128)(2,1)} async-done(((bf16[1,6,1024]{2,1,0:T(8,128)(2,1)}), bf16[128,6,1024]{2,1,0:T(8,128)(2,1)}) %all-gather.3.cloned.1.call-update) | async-done | bytes 1572880 | tf_op jit(solution)/shard_map/all_gather | solution.py:74
  599.1 2.6 reshape.365
  601.7 1.4 fusion.27
  603.3 13.2 %gather_fusion.2 = f32[2048]{0:T(1024)S(1)} fusion(f32[257]{0:T(512)S(1)} %pad_maximum_fusion, s32[2048]{0:T(1024)S(1)} %broadcast_clamp_fusion), kind=kCustom, calls=%fused_computation.2 | custom fusion | bytes 24576 | tf_op jit(solution)/shard_map/gather | solution.py:71
  617.3 14.2 %psum.15 = f32[128,16]{1,0:T(8,128)S(1)} all-reduce(f32[128,16]{1,0:T(8,128)} %reshape.300), channel_id=1, replica_groups=mesh['dp'=128,'sub'=4] {'sub'}, use_global_device_ids=true, to_apply=%region_7.8 | all-reduce | flops 2048 | bytes 16384 | tf_op jit(solution)/shard_map/psum | solution.py:78
  631.6 31.1 %all-reduce.4.cloned.1.call-done = f32[128,768]{1,0:T(8,128)} async-done(((f32[128,768]{1,0:T(8,128)}), f32[128,768]{1,0:T(8,128)}) %all-reduce.4.cloned.1.call-update) | async-done | bytes 393232 | tf_op jit(solution)/shard_map/psum | solution.py:78
  667.4 1.7 gather_fusion.3
  669.3 1.5 broadcast_multiply_fusion
  670.8 17.1 %all-to-all-start.2 = ((f32[128,2,1024]{2,1,0:T(2,128)}), f32[128,2,1024]{2,1,0:T(2,128)}, u32[]{:S(2)}, u32[]{:S(2)}) async-start(f32[128,2,1024]{2,1,0:T(2,128)} %broadcast_multiply_fusion), calls=%async_computation.2 | async-start | bytes 2097152 | tf_op jit(solution)/shard_map/all_to_all | solution.py:98
  687.9 2.3 fusion.24
  690.3 356.3 %fusion = f32[8,1024]{1,0:T(8,128)S(1)} fusion(f32[768,1024]{1,0:T(8,128)} %fusion.24), kind=kCustom, calls=%all-reduce-scatter | all-reduce-scatter fusion | flops 1048577 | bytes 3180544
  1046.6 11.9 %collective-permute-start.30 = (f32[8,1024]{1,0:T(8,128)S(1)}, f32[8,1024]{1,0:T(8,128)S(1)}, u32[]{:S(2)}, u32[]{:S(2)}) collective-permute-start(f32[8,1024]{1,0:T(8,128)S(1)} %fusion), channel_id=1, source_target_pairs={{0,124},{4,128},{8,132},{12,136},{16,140},{20,144},{24,148},{28,15... | collective-permute-start | bytes 98312
  1058.5 7.3 collective-permute-start.31
  1065.8 10.7 collective-permute-start.29
  1076.5 1.3 collective-permute-start.28
  1077.8 1.3 collective-permute-start.27
  1085.7 10.7 collective-permute-start.21
  1096.5 4.0 collective-permute-start.20
  1100.5 2.8 collective-permute-start.19
  1103.4 2.7 collective-permute-start.18
  1107.4 1.8 collective-permute-start.16
  1109.3 4.8 collective-permute-start.15
  1116.2 2.8 collective-permute-start.14
  1119.0 1.4 collective-permute-start.13
  1120.4 3.0 collective-permute-start.12
  1123.5 2.8 collective-permute-start.11
  1126.3 3.2 collective-permute-start.10
  1129.5 4.3 collective-permute-start.9
  1133.8 1.9 collective-permute-start.8
  1135.7 2.3 collective-permute-start.7
  1138.0 2.8 collective-permute-start.6
  1141.6 1.9 collective-permute-start.5
  1144.1 3.1 scatter_custom_fusion.2
  1147.2 4.0 collective-permute-start.4
  1151.2 2.8 collective-permute-start.3
  1154.1 4.0 collective-permute-start.2
  1158.1 3.1 collective-permute-start.1
  1161.2 2.4 collective-permute-start
  1164.5 3.4 collective-permute-done
  1168.0 7.3 concatenate.4
  1175.9 1.9 reshape.303
  (177 shorter events, 30.8 us)
Async XLA Ops:
  7.2 69.3 %copy-start = (bf16[128,1024]{1,0:T(8,128)(2,1)S(1)}, bf16[128,1024]{1,0:T(8,128)(2,1)}, u32[]{:S(2)}) copy-start(bf16[128,1024]{1,0:T(8,128)(2,1)} %param.5) | copy-start | bytes 786436
  7.2 591.9 %all-gather.3.cloned.1.call-start = ((), (), s32[]{:S(2)}) async-start(), calls=%async_computation.4 | async-start | bytes 2113536 | tf_op jit(solution)/shard_map/all_gather | solution.py:74
  11.9 46.0 %copy-start.1 = (bf16[16,1024]{1,0:T(8,128)(2,1)S(1)}, bf16[16,1024]{1,0:T(8,128)(2,1)}, u32[]{:S(2)}) copy-start(bf16[16,1024]{1,0:T(8,128)(2,1)} %param.7) | copy-start | bytes 98308
  60.6 38.7 %all-to-all-start.1 = ((bf16[128,2,1024]{2,1,0:T(2,128)(2,1)}), bf16[128,2,1024]{2,1,0:T(2,128)(2,1)S(1)}, u32[]{:S(2)}, u32[]{:S(2)}) async-start(bf16[128,2,1024]{2,1,0:T(2,128)(2,1)} %broadcast_select_fusion), calls=%async_computation.1 | async-start | bytes 1048576 | tf_op jit(solution)/shard_map/all_to_all | solution.py:62
  67.6 595.1 %all-reduce.4.cloned.1.call-start = ((), (), s32[]{:S(2)}) async-start(), calls=%async_computation.3 | async-start | bytes 786432 | tf_op jit(solution)/shard_map/psum | solution.py:78
  603.3 28.1 %copy-start.34 = (s32[128]{0:T(128)S(1)}, s32[128]{0:T(128)}, u32[]{:S(2)}) copy-start(s32[128]{0:T(128)} %param.9) | copy-start | bytes 1540
  616.5 52.8 %copy-start.3 = (f32[128,2,1024]{2,1,0:T(2,128)S(1)}, f32[128,2,1024]{2,1,0:T(2,128)}, u32[]{:S(2)}) copy-start(f32[128,2,1024]{2,1,0:T(2,128)} %reshape.304) | copy-start | bytes 3145732
  670.8 505.1 %all-to-all-start.2 = ((f32[128,2,1024]{2,1,0:T(2,128)}), f32[128,2,1024]{2,1,0:T(2,128)}, u32[]{:S(2)}, u32[]{:S(2)}) async-start(f32[128,2,1024]{2,1,0:T(2,128)} %broadcast_multiply_fusion), calls=%async_computation.2 | async-start | bytes 2097152 | tf_op jit(solution)/shard_map/all_to_all | solution.py:98
  1046.6 33.9 %collective-permute-start.30 = (f32[8,1024]{1,0:T(8,128)S(1)}, f32[8,1024]{1,0:T(8,128)S(1)}, u32[]{:S(2)}, u32[]{:S(2)}) collective-permute-start(f32[8,1024]{1,0:T(8,128)S(1)} %fusion), channel_id=1, source_target_pairs={{0,124},{4,128},{8,132},{12,136},{16,140},{20,144},{24,148},{28,15... | collective-permute-start | bytes 98312
  1058.5 20.6 %collective-permute-start.31 = (f32[6,1024]{1,0:T(8,128)S(1)}, f32[6,1024]{1,0:T(8,128)S(1)}, u32[]{:S(2)}, u32[]{:S(2)}) collective-permute-start(f32[6,1024]{1,0:T(8,128)S(1)} %slice.26), channel_id=1, source_target_pairs={{0,128},{4,132},{8,136},{12,140},{16,144},{20,148},{24,152},{28,15... | collective-permute-start | bytes 73736
  1065.8 15.9 %collective-permute-start.29 = (f32[8,1024]{1,0:T(8,128)S(1)}, f32[8,1024]{1,0:T(8,128)S(1)}, u32[]{:S(2)}, u32[]{:S(2)}) collective-permute-start(f32[8,1024]{1,0:T(8,128)S(1)} %fusion), channel_id=1, source_target_pairs={{0,120},{4,124},{8,128},{12,132},{16,136},{20,140},{24,144},{28,14... | collective-permute-start | bytes 98312
  1076.5 6.5 collective-permute-start.28
  1077.8 6.5 collective-permute-start.27
  1079.1 6.5 collective-permute-start.26
  1080.4 16.0 %collective-permute-start.25 = (f32[8,1024]{1,0:T(8,128)S(1)}, f32[8,1024]{1,0:T(8,128)S(1)}, u32[]{:S(2)}, u32[]{:S(2)}) collective-permute-start(f32[8,1024]{1,0:T(8,128)S(1)} %fusion), channel_id=1, source_target_pairs={{0,104},{4,108},{8,112},{12,116},{16,120},{20,124},{24,128},{28,13... | collective-permute-start | bytes 98312
  1081.7 18.7 %collective-permute-start.24 = (f32[8,1024]{1,0:T(8,128)S(1)}, f32[8,1024]{1,0:T(8,128)S(1)}, u32[]{:S(2)}, u32[]{:S(2)}) collective-permute-start(f32[8,1024]{1,0:T(8,128)S(1)} %fusion), channel_id=1, source_target_pairs={{0,100},{4,104},{8,108},{12,112},{16,116},{20,120},{24,124},{28,12... | collective-permute-start | bytes 98312
  1083.1 20.3 %collective-permute-start.23 = (f32[8,1024]{1,0:T(8,128)S(1)}, f32[8,1024]{1,0:T(8,128)S(1)}, u32[]{:S(2)}, u32[]{:S(2)}) collective-permute-start(f32[8,1024]{1,0:T(8,128)S(1)} %fusion), channel_id=1, source_target_pairs={{0,96},{4,100},{8,104},{12,108},{16,112},{20,116},{24,120},{28,124... | collective-permute-start | bytes 98312
  1084.4 21.7 %collective-permute-start.22 = (f32[8,1024]{1,0:T(8,128)S(1)}, f32[8,1024]{1,0:T(8,128)S(1)}, u32[]{:S(2)}, u32[]{:S(2)}) collective-permute-start(f32[8,1024]{1,0:T(8,128)S(1)} %fusion), channel_id=1, source_target_pairs={{0,92},{4,96},{8,100},{12,104},{16,108},{20,112},{24,116},{28,120}... | collective-permute-start | bytes 98312
  1085.7 55.2 %copy-start.4 = (f32[8,1024]{1,0:T(8,128)}, f32[8,1024]{1,0:T(8,128)S(1)}, u32[]{:S(2)}) copy-start(f32[8,1024]{1,0:T(8,128)S(1)} %collective-permute-done.26) | copy-start | bytes 98308
  1085.7 21.7 %collective-permute-start.21 = (f32[8,1024]{1,0:T(8,128)S(1)}, f32[8,1024]{1,0:T(8,128)S(1)}, u32[]{:S(2)}, u32[]{:S(2)}) collective-permute-start(f32[8,1024]{1,0:T(8,128)S(1)} %fusion), channel_id=1, source_target_pairs={{0,88},{4,92},{8,96},{12,100},{16,104},{20,108},{24,112},{28,116},... | collective-permute-start | bytes 98312
  1096.4 44.4 %copy-start.6 = (f32[8,1024]{1,0:T(8,128)}, f32[8,1024]{1,0:T(8,128)S(1)}, u32[]{:S(2)}) copy-start(f32[8,1024]{1,0:T(8,128)S(1)} %collective-permute-done.25) | copy-start | bytes 98308
  1096.5 12.8 %collective-permute-start.20 = (f32[8,1024]{1,0:T(8,128)S(1)}, f32[8,1024]{1,0:T(8,128)S(1)}, u32[]{:S(2)}, u32[]{:S(2)}) collective-permute-start(f32[8,1024]{1,0:T(8,128)S(1)} %fusion), channel_id=1, source_target_pairs={{0,84},{4,88},{8,92},{12,96},{16,100},{20,104},{24,108},{28,112},{... | collective-permute-start | bytes 98312
  1100.5 40.4 %copy-start.8 = (f32[8,1024]{1,0:T(8,128)}, f32[8,1024]{1,0:T(8,128)S(1)}, u32[]{:S(2)}) copy-start(f32[8,1024]{1,0:T(8,128)S(1)} %collective-permute-done.24) | copy-start | bytes 98308
  1100.5 15.6 %collective-permute-start.19 = (f32[8,1024]{1,0:T(8,128)S(1)}, f32[8,1024]{1,0:T(8,128)S(1)}, u32[]{:S(2)}, u32[]{:S(2)}) collective-permute-start(f32[8,1024]{1,0:T(8,128)S(1)} %fusion), channel_id=1, source_target_pairs={{0,80},{4,84},{8,88},{12,92},{16,96},{20,100},{24,104},{28,108},{3... | collective-permute-start | bytes 98312
  1103.4 37.5 %copy-start.10 = (f32[8,1024]{1,0:T(8,128)}, f32[8,1024]{1,0:T(8,128)S(1)}, u32[]{:S(2)}) copy-start(f32[8,1024]{1,0:T(8,128)S(1)} %collective-permute-done.23) | copy-start | bytes 98308
  1103.4 15.6 %collective-permute-start.18 = (f32[8,1024]{1,0:T(8,128)S(1)}, f32[8,1024]{1,0:T(8,128)S(1)}, u32[]{:S(2)}, u32[]{:S(2)}) collective-permute-start(f32[8,1024]{1,0:T(8,128)S(1)} %fusion), channel_id=1, source_target_pairs={{0,76},{4,80},{8,84},{12,88},{16,92},{20,96},{24,100},{28,104},{32... | collective-permute-start | bytes 98312
  1106.1 34.8 %copy-start.12 = (f32[8,1024]{1,0:T(8,128)}, f32[8,1024]{1,0:T(8,128)S(1)}, u32[]{:S(2)}) copy-start(f32[8,1024]{1,0:T(8,128)S(1)} %collective-permute-done.22) | copy-start | bytes 98308
  1106.1 14.3 %collective-permute-start.17 = (f32[8,1024]{1,0:T(8,128)S(1)}, f32[8,1024]{1,0:T(8,128)S(1)}, u32[]{:S(2)}, u32[]{:S(2)}) collective-permute-start(f32[8,1024]{1,0:T(8,128)S(1)} %fusion), channel_id=1, source_target_pairs={{0,72},{4,76},{8,80},{12,84},{16,88},{20,92},{24,96},{28,100},{32,... | collective-permute-start | bytes 98312
  1107.4 33.5 %copy-start.14 = (f32[8,1024]{1,0:T(8,128)}, f32[8,1024]{1,0:T(8,128)S(1)}, u32[]{:S(2)}) copy-start(f32[8,1024]{1,0:T(8,128)S(1)} %collective-permute-done.21) | copy-start | bytes 98308
  1107.4 16.0 %collective-permute-start.16 = (f32[8,1024]{1,0:T(8,128)S(1)}, f32[8,1024]{1,0:T(8,128)S(1)}, u32[]{:S(2)}, u32[]{:S(2)}) collective-permute-start(f32[8,1024]{1,0:T(8,128)S(1)} %fusion), channel_id=1, source_target_pairs={{0,68},{4,72},{8,76},{12,80},{16,84},{20,88},{24,92},{28,96},{32,1... | collective-permute-start | bytes 98312
  1109.3 31.6 %copy-start.16 = (f32[8,1024]{1,0:T(8,128)}, f32[8,1024]{1,0:T(8,128)S(1)}, u32[]{:S(2)}) copy-start(f32[8,1024]{1,0:T(8,128)S(1)} %collective-permute-done.20) | copy-start | bytes 98308
  1109.3 17.0 %collective-permute-start.15 = (f32[8,1024]{1,0:T(8,128)S(1)}, f32[8,1024]{1,0:T(8,128)S(1)}, u32[]{:S(2)}, u32[]{:S(2)}) collective-permute-start(f32[8,1024]{1,0:T(8,128)S(1)} %fusion), channel_id=1, source_target_pairs={{0,64},{4,68},{8,72},{12,76},{16,80},{20,84},{24,88},{28,92},{32,9... | collective-permute-start | bytes 98312
  1116.2 24.7 %copy-start.18 = (f32[8,1024]{1,0:T(8,128)}, f32[8,1024]{1,0:T(8,128)S(1)}, u32[]{:S(2)}) copy-start(f32[8,1024]{1,0:T(8,128)S(1)} %collective-permute-done.19) | copy-start | bytes 98308
  1116.2 13.3 %collective-permute-start.14 = (f32[8,1024]{1,0:T(8,128)S(1)}, f32[8,1024]{1,0:T(8,128)S(1)}, u32[]{:S(2)}, u32[]{:S(2)}) collective-permute-start(f32[8,1024]{1,0:T(8,128)S(1)} %fusion), channel_id=1, source_target_pairs={{0,60},{4,64},{8,68},{12,72},{16,76},{20,80},{24,84},{28,88},{32,9... | collective-permute-start | bytes 98312
  1119.0 14.8 %collective-permute-start.13 = (f32[8,1024]{1,0:T(8,128)S(1)}, f32[8,1024]{1,0:T(8,128)S(1)}, u32[]{:S(2)}, u32[]{:S(2)}) collective-permute-start(f32[8,1024]{1,0:T(8,128)S(1)} %fusion), channel_id=1, source_target_pairs={{0,56},{4,60},{8,64},{12,68},{16,72},{20,76},{24,80},{28,84},{32,8... | collective-permute-start | bytes 98312
  1120.4 15.3 %collective-permute-start.12 = (f32[8,1024]{1,0:T(8,128)S(1)}, f32[8,1024]{1,0:T(8,128)S(1)}, u32[]{:S(2)}, u32[]{:S(2)}) collective-permute-start(f32[8,1024]{1,0:T(8,128)S(1)} %fusion), channel_id=1, source_target_pairs={{0,52},{4,56},{8,60},{12,64},{16,68},{20,72},{24,76},{28,80},{32,8... | collective-permute-start | bytes 98312
  1123.5 14.5 %collective-permute-start.11 = (f32[8,1024]{1,0:T(8,128)S(1)}, f32[8,1024]{1,0:T(8,128)S(1)}, u32[]{:S(2)}, u32[]{:S(2)}) collective-permute-start(f32[8,1024]{1,0:T(8,128)S(1)} %fusion), channel_id=1, source_target_pairs={{0,48},{4,52},{8,56},{12,60},{16,64},{20,68},{24,72},{28,76},{32,8... | collective-permute-start | bytes 98312
  1126.3 14.5 %collective-permute-start.10 = (f32[8,1024]{1,0:T(8,128)S(1)}, f32[8,1024]{1,0:T(8,128)S(1)}, u32[]{:S(2)}, u32[]{:S(2)}) collective-permute-start(f32[8,1024]{1,0:T(8,128)S(1)} %fusion), channel_id=1, source_target_pairs={{0,44},{4,48},{8,52},{12,56},{16,60},{20,64},{24,68},{28,72},{32,7... | collective-permute-start | bytes 98312
  1129.5 17.7 %collective-permute-start.9 = (f32[8,1024]{1,0:T(8,128)S(1)}, f32[8,1024]{1,0:T(8,128)}, u32[]{:S(2)}, u32[]{:S(2)}) collective-permute-start(f32[8,1024]{1,0:T(8,128)S(1)} %fusion), channel_id=1, source_target_pairs={{0,40},{4,44},{8,48},{12,52},{16,56},{20,60},{24,64},{28,68},{32,7... | collective-permute-start | bytes 98312
  1133.8 17.4 %collective-permute-start.8 = (f32[8,1024]{1,0:T(8,128)S(1)}, f32[8,1024]{1,0:T(8,128)}, u32[]{:S(2)}, u32[]{:S(2)}) collective-permute-start(f32[8,1024]{1,0:T(8,128)S(1)} %fusion), channel_id=1, source_target_pairs={{0,36},{4,40},{8,44},{12,48},{16,52},{20,56},{24,60},{28,64},{32,6... | collective-permute-start | bytes 98312
  1135.7 18.3 %collective-permute-start.7 = (f32[8,1024]{1,0:T(8,128)S(1)}, f32[8,1024]{1,0:T(8,128)}, u32[]{:S(2)}, u32[]{:S(2)}) collective-permute-start(f32[8,1024]{1,0:T(8,128)S(1)} %fusion), channel_id=1, source_target_pairs={{0,32},{4,36},{8,40},{12,44},{16,48},{20,52},{24,56},{28,60},{32,6... | collective-permute-start | bytes 98312
  1138.0 20.0 %collective-permute-start.6 = (f32[8,1024]{1,0:T(8,128)S(1)}, f32[8,1024]{1,0:T(8,128)}, u32[]{:S(2)}, u32[]{:S(2)}) collective-permute-start(f32[8,1024]{1,0:T(8,128)S(1)} %fusion), channel_id=1, source_target_pairs={{0,28},{4,32},{8,36},{12,40},{16,44},{20,48},{24,52},{28,56},{32,6... | collective-permute-start | bytes 98312
  1141.6 19.6 %collective-permute-start.5 = (f32[8,1024]{1,0:T(8,128)S(1)}, f32[8,1024]{1,0:T(8,128)}, u32[]{:S(2)}, u32[]{:S(2)}) collective-permute-start(f32[8,1024]{1,0:T(8,128)S(1)} %fusion), channel_id=1, source_target_pairs={{0,24},{4,28},{8,32},{12,36},{16,40},{20,44},{24,48},{28,52},{32,5... | collective-permute-start | bytes 98312
  1147.2 17.2 %collective-permute-start.4 = (f32[8,1024]{1,0:T(8,128)S(1)}, f32[8,1024]{1,0:T(8,128)S(1)}, u32[]{:S(2)}, u32[]{:S(2)}) collective-permute-start(f32[8,1024]{1,0:T(8,128)S(1)} %fusion), channel_id=1, source_target_pairs={{0,20},{4,24},{8,28},{12,32},{16,36},{20,40},{24,44},{28,48},{32,5... | collective-permute-start | bytes 98312
  1151.2 13.2 %collective-permute-start.3 = (f32[8,1024]{1,0:T(8,128)S(1)}, f32[8,1024]{1,0:T(8,128)S(1)}, u32[]{:S(2)}, u32[]{:S(2)}) collective-permute-start(f32[8,1024]{1,0:T(8,128)S(1)} %fusion), channel_id=1, source_target_pairs={{0,16},{4,20},{8,24},{12,28},{16,32},{20,36},{24,40},{28,44},{32,4... | collective-permute-start | bytes 98312
  1154.1 10.4 collective-permute-start.2
  1158.1 6.4 collective-permute-start.1
  1161.2 6.7 collective-permute-start
  (23 other events, 459.2 us)
Sparse Core Ops, SparseCore 0:
  10.1 588.9 all-gather.2
  603.2 59.4 all-reduce.3
where the time goes:
time: 1190 us
  waiting for transfers between devices  555 us (47%)
  blocking collectives  405 us (34%)
  starting transfers between devices  134 us (11%)
  local copies, waits for them, and re-layouts  55.2 us (5%)
  other arithmetic  16.1 us (1%)
  between operations  15.9 us (1%)
    all_gather x1, waiting for transfers between devices, body(): all_passages = lax.all_gather(passages, 'dp', axis=0, tiled=True)  500 us
    unnamed x1, blocking collectives  356 us
    unnamed x32, starting transfers between devices  110 us
    all_to_all x1, blocking collectives, body(): lax.all_to_all(send_ids.reshape(peer_count, capacity), 'dp', split_axis=0...  34.1 us
    psum x1, waiting for transfers between devices, body(): score_sums, pos_sums = lax.psum((score_part, pos_part), 'sub')  31.1 us
  transfers between devices with their start and end apart: 36, of which 4 were waited for; matrix products, arithmetic and copies ran while one was open for 35% of the time, Pallas kernels for 0%

commit v1 on v0

v1 whole, which is shorter than its diff:
```python
import functools

import jax
import jax.numpy as jnp
from jax import lax
from jax.experimental import pallas as pl
from jax.experimental.pallas import tpu as pltpu
from jax.sharding import PartitionSpec as P

MESH = pl.DeviceIdType.MESH
F32 = jnp.float32
BF16 = jnp.bfloat16
NZ = 16
NC = 8
SCALE = 50.0


def iota(shape, dim):
    return lax.broadcasted_iota(jnp.int32, shape, dim)


def dot(a, b, ca, cb):
    return lax.dot_general(a, b, (((ca,), (cb,)), ((), ())), preferred_element_type=F32)


def split(v):
    hi = v.astype(BF16)
    return hi, (v - hi.astype(F32)).astype(BF16)


def kernel(
    q_ref, p_ref, b_ref, ids_ref, cnt_ref,
    loss_ref, qg_ref, pg_ref, bg_ref,
    q2, bcol, pz, pb32, pz32, p32, pall,
    sel, idt, id_recv, smat, qs_send, qs_recv, pk_send, pk_recv,
    spart, sc_recv, ss_all, st_send, st_recv, pos_m, pos_e, w_all, lt_all, cf, cf_recv,
    pg_part, xg_recv, zp_part, zp_r, zp_l, bk_part, bk_r, bk_l, qx_send, qx_recv,
    q_sem, bg_s, bg_r, pg_s, pg_r, qs_s, qs_r, id_s, id_r, pk_s, pk_r, cf_s, cf_r,
    x_s, x_r, sc_s, sc_r, ss_s, ss_r, st_sem, w_s, w_r, lt_s, lt_r, xg_s, xg_r,
    br_s, br_r, pr_s, pr_r, qx_sem,
):
    dp = lax.axis_index("dp")
    j = lax.axis_index("sub")
    z = lax.div(dp, NC)
    c = lax.rem(dp, NC)
    x = lax.div(c, 2)
    yl = lax.rem(c, 2)
    yh = lax.div(j, 2)
    core = lax.rem(j, 2)
    right = lax.rem(z + 1, NZ) * NC + c
    left = lax.rem(z + NZ - 1, NZ) * NC + c
    mate = dp + 1 - 2 * yl
    plane = [z * NC + lax.rem(c + d, NC) for d in range(1, NC)]
    plane_c = [lax.rem(c + d, NC) for d in range(1, NC)]
    xs = [lax.rem(x + d, 4) for d in range(1, 4)]
    xdp = [z * NC + v * 2 + yl for v in xs]
    subs = [j + 1 - 2 * core, j + 2 - 4 * yh, 3 - j]

    def remote(src, dst, ssem, rsem, to_dp, to_sub):
        return pltpu.make_async_remote_copy(
            src_ref=src, dst_ref=dst, send_sem=ssem, recv_sem=rsem,
            device_id=(to_dp, to_sub), device_id_type=MESH,
        )

    barrier = pltpu.get_barrier_semaphore()
    for to_dp in (right, left, *plane):
        pl.semaphore_signal(barrier, inc=1, device_id=(to_dp, j), device_id_type=MESH)
    for to_sub in subs:
        pl.semaphore_signal(barrier, inc=1, device_id=(dp, to_sub), device_id_type=MESH)
    pl.semaphore_wait(barrier, 12)

    sent = []

    def go(copy):
        copy.start()
        sent.append(copy)
        return copy

    q_copy = go(remote(q_ref, q2.at[yl], q_sem.at[0], q_sem.at[1], mate, j))

    def gather_step(t, buf, own, ssem, rsem, log):
        if t > 0:
            log[t - 1][0].wait_recv()
            if t - 1 < NZ // 2 - 1:
                log[t - 1][1].wait_recv()
        if t == NZ // 2:
            return
        src = lax.rem(z + NZ - t, NZ)
        row = [go(remote(own if t == 0 else buf.at[src], buf.at[src], ssem.at[t], rsem.at[t], right, j))]
        if t < NZ // 2 - 1:
            src = lax.rem(z + t, NZ)
            k = NZ // 2 + t
            row.append(go(remote(own if t == 0 else buf.at[src], buf.at[src], ssem.at[k], rsem.at[k], left, j)))
        log.append(row)

    b_log, p_log = [], []
    p_own = p_ref[...].astype(F32)
    for k in range(8):
        pb32[k * 6 : k * 6 + 6, :] = p_own[:, k * 128 : (k + 1) * 128]
    pz[z] = pb32[...].astype(BF16)
    gather_step(0, pz, pz.at[z], pg_s, pg_r, p_log)
    gather_step(0, bcol, b_ref, bg_s, bg_r, b_log)
    bcol[z] = b_ref[...]
    q2[yl] = q_ref[...]

    def ring(t):
        gather_step(t, pz, None, pg_s, pg_r, p_log)
        gather_step(t, bcol, None, bg_s, bg_r, b_log)

    lane = iota((128, 128), 1)
    row = iota((128, 128), 0)
    eye = lane == row
    ids = ids_ref[...]
    owner = lax.shift_right_arithmetic(ids, 4)
    place = jnp.where(
        ids >= 0, (owner & 7) * 16 + lax.shift_right_arithmetic(owner, 3), -1
    )
    local = (ids & 15).astype(F32)
    many = jnp.zeros((128, 128), F32)
    w_sum = jnp.zeros((128, 128), F32)
    w_max = jnp.full((128, 128), -1.0, F32)
    for k in range(16):
        hit = place[:, k : k + 1] == lane
        w_k = local[:, k : k + 1]
        many = many + jnp.where(hit, 1.0, 0.0)
        w_sum = w_sum + jnp.where(hit, w_k, 0.0)
        w_max = jnp.maximum(w_max, jnp.where(hit, w_k, -1.0))
    ring(1)
    below = jnp.where(lane < row, 1.0, 0.0).astype(BF16)
    before = dot(below, many.astype(BF16), 1, 0)
    twice = (many > 1.5) & (before < 0.5)
    first = (many > 0.5) & (before < 0.5)
    second = ((many > 0.5) & (before > 0.5)) | twice
    w_second = jnp.where(twice, w_sum - w_max, w_max)
    id0 = jnp.sum(jnp.where(first, w_max + 1.0, 0.0), 0, keepdims=True) - 1.0
    id1 = jnp.sum(jnp.where(second, w_second + 1.0, 0.0), 0, keepdims=True) - 1.0
    sel[0] = jnp.where(first, 1.0, 0.0)
    sel[1] = jnp.where(second, 1.0, 0.0)
    tile_row = iota((8, 128), 0)
    idt[...] = jnp.where(tile_row == 0, id0, jnp.where(tile_row == 1, id1, -1.0))
    ring(2)
    id_copies = [go(remote(idt, id_recv.at[c], id_s.at[d], id_r.at[d], plane[d], j)) for d in range(7)]
    id_recv[c] = idt[...]
    for r in range(2):
        picked_q = dot(sel[r].astype(BF16), q_ref[...], 0, 0).astype(BF16)
        for k in range(NC):
            qs_send[k, r * 16 : (r + 1) * 16, :] = picked_q[k * 16 : (k + 1) * 16]
    qs_copies = [go(remote(qs_send.at[plane_c[d]], qs_recv.at[c], qs_s.at[d], qs_r.at[d], plane[d], j)) for d in range(7)]
    qs_recv[c] = qs_send[c]
    for t in range(3, NZ // 2 + 1):
        ring(t)

    pz32[...] = pz[...].reshape(NZ * 48, 128).astype(F32)
    for zz in range(NZ):
        for k in range(8):
            at = zz * 48 + k * 6
            p32[zz * 6 : zz * 6 + 6, k * 128 : (k + 1) * 128] = pz32[at : at + 6, :]
    pall[x] = p32[...].astype(BF16)
    x_copies = [go(remote(pall.at[x], pall.at[x], x_s.at[d], x_r.at[d], xdp[d], j)) for d in range(3)]

    for copy in id_copies:
        copy.wait_recv()
    lane16 = iota((16, 128), 1)
    mine = lane16 == c * 16 + iota((16, 128), 0)

    def to_column(tile_rows):
        return jnp.sum(jnp.where(mine, tile_rows, 0.0), 1, keepdims=True)

    bank_lane = iota((16, 256), 1).astype(F32) - iota((16, 256), 0).astype(F32) * 16.0
    for k in range(NC):
        for r in range(2):
            w_col = to_column(id_recv[k, r : r + 1, :])
            hot = (bank_lane == w_col) & (w_col > -0.5)
            at = k * 32 + r * 16
            smat[at : at + 16, :] = jnp.where(hot, 1.0, 0.0)
    picked_b = dot(smat[...].astype(BF16), bcol[...].reshape(256, 1024), 1, 0)
    pk_send[...] = picked_b.astype(BF16).reshape(NC, 32, 1024)
    pk_copies = [go(remote(pk_send.at[plane_c[d]], pk_recv.at[c], pk_s.at[d], pk_r.at[d], plane[d], j)) for d in range(7)]
    pk_recv[c] = pk_send[c]

    q_copy.wait_recv()
    for copy in x_copies:
        copy.wait_recv()
    part = dot(q2[...].reshape(256, 1024), pall[...].reshape(384, 1024), 1, 1)
    spart[...] = part.reshape(4, 64, 384)
    sc_copies = [go(remote(spart.at[subs[d]], sc_recv.at[d], sc_s.at[d], sc_r.at[d], dp, subs[d])) for d in range(3)]

    for copy in pk_copies:
        copy.wait_recv()

    def slots(ref, r):
        return ref[:, r * 16 : (r + 1) * 16, :].reshape(128, 1024)

    def col_to_row(v):
        return jnp.sum(jnp.where(eye, v, 0.0), 0, keepdims=True)

    def row_to_col(v):
        return jnp.sum(jnp.where(eye, v, 0.0), 1, keepdims=True)

    rows = []
    for r in range(2):
        prod = slots(qs_send, r).astype(F32) * slots(pk_recv, r).astype(F32)
        rows.append(col_to_row(jnp.sum(prod, 1, keepdims=True)))
    ss_all[j] = jnp.where(tile_row == 0, rows[0], jnp.where(tile_row == 1, rows[1], 0.0))
    ss_copies = [go(remote(ss_all.at[j], ss_all.at[j], ss_s.at[d], ss_r.at[d], dp, subs[d])) for d in range(3)]
    inv_col = 1.0 / row_to_col(cnt_ref[...].astype(F32))
    for copy in ss_copies:
        copy.wait_recv()
    ss = (((ss_all[0] + ss_all[1]) + ss_all[2]) + ss_all[3]) * SCALE
    has = [sel[r] > 0.5 for r in range(2)]
    low = [jnp.where(has[r], ss[r : r + 1], -jnp.inf) for r in range(2)]
    p_max = jnp.max(jnp.maximum(low[0], low[1]), 1, keepdims=True)
    p_exp = jnp.sum(jnp.exp(low[0] - p_max) + jnp.exp(low[1] - p_max), 1, keepdims=True)
    p_sum = jnp.sum(
        jnp.where(has[0], ss[0:1], 0.0) + jnp.where(has[1], ss[1:2], 0.0), 1, keepdims=True
    )
    pos_m[...] = jnp.broadcast_to(p_max, (128, 128))
    pos_e[...] = jnp.broadcast_to(p_exp, (128, 128))

    for copy in sc_copies:
        copy.wait_recv()
    scores = (spart[j] + sc_recv[0] + sc_recv[1] + sc_recv[2]) * SCALE
    start = pl.multiple_of(core * 64, 64)
    m_col = jnp.max(scores, 1, keepdims=True)
    here = yl == yh
    pm = jnp.where(here, pos_m[pl.ds(start, 64), 0:1], m_col)
    pe = jnp.where(here, pos_e[pl.ds(start, 64), 0:1], 0.0)
    m_all = jnp.maximum(m_col, pm)
    s_all = jnp.sum(jnp.exp(scores - m_all), 1, keepdims=True) + pe * jnp.exp(pm - m_all)
    eye64 = iota((64, 128), 1) == iota((64, 128), 0)
    m_row = jnp.sum(jnp.where(eye64, m_all, 0.0), 0, keepdims=True)
    s_row = jnp.sum(jnp.where(eye64, s_all, 0.0), 0, keepdims=True)
    st_send[...] = jnp.where(tile_row == 0, m_row, s_row)
    st_copy = go(remote(st_send, st_recv, st_sem.at[0], st_sem.at[1], mate, j))
    st_copy.wait_recv()
    m_two = jnp.sum(jnp.where(eye64, st_recv[0:1, :], 0.0), 1, keepdims=True)
    s_two = jnp.sum(jnp.where(eye64, st_recv[1:2, :], 0.0), 1, keepdims=True)
    m_top = jnp.maximum(m_all, m_two)
    total = s_all * jnp.exp(m_all - m_top) + s_two * jnp.exp(m_two - m_top)
    log_total = m_top + jnp.log(total)
    w_all[j] = jnp.exp(scores - log_total).astype(BF16)
    placed = iota((64, 128), 1) == iota((64, 128), 0) + core * 64
    lt_row = jnp.sum(jnp.where(placed, log_total, 0.0), 0, keepdims=True)
    lt_all[j] = jnp.broadcast_to(lt_row, (8, 128))
    lt_copies = [go(remote(lt_all.at[j], lt_all.at[j], lt_s.at[d], lt_r.at[d], dp, subs[d])) for d in range(3)]
    w_copies = [go(remote(w_all.at[j], w_all.at[j], w_s.at[d], w_r.at[d], dp, subs[d])) for d in range(3)]

    for copy in lt_copies:
        copy.wait_recv()
    lt_col = row_to_col(lt_all[yl * 2, 0:1, :] + lt_all[yl * 2 + 1, 0:1, :])
    coef = []
    for r in range(2):
        lt_slot = jnp.sum(jnp.where(has[r], lt_col, 0.0), 0, keepdims=True)
        inv_slot = jnp.sum(jnp.where(has[r], inv_col, 0.0), 0, keepdims=True)
        live = jnp.sum(sel[r], 0, keepdims=True) > 0.5
        coef.append(jnp.where(live, jnp.exp(jnp.where(live, ss[r : r + 1] - lt_slot, 0.0)) - inv_slot, 0.0))
    cf[...] = jnp.where(tile_row == 0, coef[0], jnp.where(tile_row == 1, coef[1], 0.0))
    cf_copies = [go(remote(cf, cf_recv.at[c], cf_s.at[d], cf_r.at[d], plane[d], j)) for d in range(7)]
    cf_recv[c] = cf[...]
    loss_ref[...] = col_to_row(lt_col - p_sum * inv_col)

    for copy in w_copies:
        copy.wait_recv()
    weights = w_all[...].reshape(256, 384)
    pg_part[...] = dot(weights, q2[...].reshape(256, 1024), 0, 0).reshape(4, 96, 1024)
    xg_copies = [go(remote(pg_part.at[xs[d]], xg_recv.at[d], xg_s.at[d], xg_r.at[d], xdp[d], j)) for d in range(3)]

    p_half = pall[...].reshape(384, 1024)
    theirs = jnp.concatenate([w_all[2 - yl * 2], w_all[3 - yl * 2]], 0)
    qx_send[...] = dot(theirs, p_half, 1, 0)
    qx_copy = go(remote(qx_send, qx_recv, qx_sem.at[0], qx_sem.at[1], mate, j))

    def scatter_step(t, part_ref, buf_r, buf_l, ssem, rsem, log):
        half = NZ // 2
        if t > 0:
            log[t - 1][0].wait_recv()
            if t - 1 < half - 1:
                log[t - 1][1].wait_recv()
        if t == half:
            return
        to_r = lax.rem(z + half - t, NZ)
        to_l = lax.rem(z + half + 1 + t, NZ)
        if t > 0:
            buf_r[t - 1] += part_ref[to_r]
            if t < half - 1:
                buf_l[t - 1] += part_ref[to_l]
        src = part_ref.at[to_r] if t == 0 else buf_r.at[t - 1]
        got = [go(remote(src, buf_r.at[t], ssem.at[t], rsem.at[t], right, j))]
        if t < half - 1:
            src = part_ref.at[to_l] if t == 0 else buf_l.at[t - 1]
            got.append(go(remote(src, buf_l.at[t], ssem.at[half + t], rsem.at[half + t], left, j)))
        log.append(got)

    br_log, pr_log = [], []
    for copy in cf_copies:
        copy.wait_recv()
    cols = []
    for k in range(NC):
        for r in range(2):
            cols.append(to_column(cf_recv[k, r : r + 1, :]))
    hi, lo = split(smat[...] * jnp.concatenate(cols, 0))
    for copy in qs_copies:
        copy.wait_recv()
    asked = qs_recv[...].reshape(256, 1024)
    bk_part[...] = (dot(hi, asked, 0, 0) + dot(lo, asked, 0, 0)).reshape(NZ, 16, 1024)
    scatter_step(0, bk_part, bk_r, bk_l, br_s, br_r, br_log)

    own = jnp.concatenate([w_all[yl * 2], w_all[yl * 2 + 1]], 0)
    mine_g = dot(own, p_half, 1, 0)
    for r in range(2):
        hi, lo = split(sel[r] * coef[r])
        rows_b = slots(pk_recv, r)
        mine_g = mine_g + dot(hi, rows_b, 1, 0) + dot(lo, rows_b, 1, 0)
    qg_ref[...] = mine_g
    scatter_step(1, bk_part, bk_r, bk_l, br_s, br_r, br_log)
    scatter_step(2, bk_part, bk_r, bk_l, br_s, br_r, br_log)
    scatter_step(3, bk_part, bk_r, bk_l, br_s, br_r, br_log)

    for copy in xg_copies:
        copy.wait_recv()
    p32[...] = pg_part[x] + xg_recv[0] + xg_recv[1] + xg_recv[2]
    zp_part[...] = jnp.zeros((NZ, 8, 1024), F32)
    for zz in range(NZ):
        zp_part[zz, 0:6, :] = p32[zz * 6 : zz * 6 + 6, :]
    scatter_step(0, zp_part, zp_r, zp_l, pr_s, pr_r, pr_log)
    for t in range(1, NZ // 2 + 1):
        if t + 3 <= NZ // 2:
            scatter_step(t + 3, bk_part, bk_r, bk_l, br_s, br_r, br_log)
        scatter_step(t, zp_part, zp_r, zp_l, pr_s, pr_r, pr_log)
    last = NZ // 2 - 1
    bg_ref[...] = SCALE * (bk_part[z] + bk_r[last] + bk_l[last - 1])
    pg_ref[...] = SCALE * (zp_part[z] + zp_r[last] + zp_l[last - 1])[0:6]
    qx_copy.wait_recv()
    qg_ref[...] = SCALE * (qg_ref[...] + qx_recv[...])
    for copy in sent:
        copy.wait_send()


def body(queries, passages, positive_bank, positive_ids, positive_counts):
    vmem = pl.BlockSpec(memory_space=pltpu.VMEM)
    dma = pltpu.SemaphoreType.DMA
    half = NZ - 1

    def buf(*shape):
        return pltpu.VMEM(shape, F32)

    def buf16(*shape):
        return pltpu.VMEM(shape, BF16)

    scratch = [
        buf16(2, 128, 1024), buf16(NZ, 16, 1024), buf16(NZ, 48, 128), buf(48, 128), buf(NZ * 48, 128),
        buf(96, 1024), buf16(4, 96, 1024),
        buf(2, 128, 128), buf(8, 128), buf(NC, 8, 128), buf(256, 256), buf16(NC, 32, 1024),
        buf16(NC, 32, 1024), buf16(NC, 32, 1024), buf16(NC, 32, 1024),
        buf(4, 64, 384), buf(3, 64, 384), buf(4, 8, 128), buf(8, 128), buf(8, 128), buf(128, 128), buf(128, 128),
        buf16(4, 64, 384), buf(4, 8, 128), buf(8, 128), buf(NC, 8, 128),
        buf(4, 96, 1024), buf(3, 96, 1024), buf(NZ, 8, 1024), buf(8, 8, 1024), buf(7, 8, 1024),
        buf(NZ, 16, 1024), buf(8, 16, 1024), buf(7, 16, 1024), buf(128, 1024), buf(128, 1024),
        dma((2,)), dma((half,)), dma((half,)), dma((half,)), dma((half,)),
        dma((7,)), dma((7,)), dma((7,)), dma((7,)), dma((7,)), dma((7,)), dma((7,)), dma((7,)),
        dma((3,)), dma((3,)), dma((3,)), dma((3,)), dma((3,)), dma((3,)), dma((2,)),
        dma((3,)), dma((3,)), dma((3,)), dma((3,)), dma((3,)), dma((3,)),
        dma((half,)), dma((half,)), dma((half,)), dma((half,)), dma((2,)),
    ]
    losses, query_grad, passage_grad, bank_grad = pl.pallas_call(
        kernel,
        out_shape=(
            jax.ShapeDtypeStruct((1, 128), F32),
            jax.ShapeDtypeStruct((128, 1024), F32),
            jax.ShapeDtypeStruct((6, 1024), F32),
            jax.ShapeDtypeStruct((16, 1024), F32),
        ),
        in_specs=[vmem] * 5,
        out_specs=(vmem,) * 4,
        scratch_shapes=scratch,
        compiler_params=pltpu.CompilerParams(
            collective_id=0, has_side_effects=True, vmem_limit_bytes=48 * 2**20
        ),
    )(queries, passages, positive_bank, positive_ids, positive_counts.reshape(1, -1))
    return losses.reshape(-1), query_grad, passage_grad, bank_grad


def solution(mesh):
    placed = (P("dp", "sub"), P("dp", "sub"), P("dp", "sub"), P("dp", None), P("dp"))
    return jax.shard_map(
        body,
        mesh=mesh,
        in_specs=placed,
        out_specs=(P("dp"), P("dp", "sub"), P("dp", "sub"), P("dp", "sub")),
        check_vma=False,
    )
```

time: 1190 us -> 124 us (0.10)
  the two profiles are of different devices: /device:TPU:4 before, /device:TPU:14 now
where the time goes in v1:
time: 124 us
  Pallas kernels  119 us (96%)
  local copies, waits for them, and re-layouts  4.32 us (3%)
    pallas_call x1, Pallas kernels, body(): pl.pallas_call(kernel, out_shape=(jax.ShapeDtypeStruct((1, 128), F32), ja...  119 us
    unnamed x13, local copies, waits for them, and re-layouts  4.32 us

profile of v1, /device:TPU:14, one launch (start us, length us, event | category | flops | bytes accessed | tf_op | source)
XLA Modules:
  0.0 123.9 jit_solution(15068956475035800883)
XLA Ops:
  0.6 0.0 copy-start.1
  0.6 0.0 copy-start.2
  0.7 0.0 copy-start.3
  0.7 0.8 copy.9.ids_ref
  1.5 0.0 copy-done.1
  1.5 0.0 copy-done.2
  1.5 0.0 copy-done.3
  1.5 0.0 copy-start
  1.5 0.9 copy-done
  2.5 118.9 %shard_map.84 = (f32[1,128]{1,0:T(1,128)S(1)}, f32[128,1024]{1,0:T(8,128)S(1)}, f32[6,1024]{1,0:T(8,128)S(1)}, f32[16,1024]{1,0:T(8,128)S(1)}) custom-call(bf16[128,1024]{1,0:T(8,128)(2,1)S(1)} %copy-done, bf16[6,1024]{1,0:T(8,128)(2,1)S(1)} %copy-done.2, bf16[16,1024]{1,0:T(8,128)(2,1)S(1)} %copy-done.1, s32[128,16]{1,0:T(8,128)S(1)} %copy.9.ids_ref, ...), custom_call_target="tpu_custom_call" | custom-call | tf_op jit(solution)/shard_map/pallas_call | solution.py:365
  121.4 0.5 copy.14
  121.9 0.8 copy.15
  122.7 0.6 copy.16
  123.3 0.6 copy.17
Async XLA Ops:
  0.6 0.8 copy-start.1
  0.6 0.8 copy-start.2
  0.7 0.8 copy-start.3
  1.5 1.0 copy-start

commit v2 on v1

v2 whole, which is shorter than its diff:
```python
import jax
import jax.numpy as jnp
from jax import lax
from jax.experimental import pallas as pl
from jax.experimental.pallas import tpu as pltpu
from jax.sharding import PartitionSpec as P

MESH = pl.DeviceIdType.MESH
F32 = jnp.float32
BF16 = jnp.bfloat16
NZ = 16
NC = 8
SCALE = 50.0


def iota(shape, dim):
    return lax.broadcasted_iota(jnp.int32, shape, dim)


def dot(a, b, ca, cb):
    return lax.dot_general(a, b, (((ca,), (cb,)), ((), ())), preferred_element_type=F32)


def split(v):
    hi = v.astype(BF16)
    return hi, (v - hi.astype(F32)).astype(BF16)


def kernel(
    q_ref, p_ref, b_ref, ids_ref, cnt_ref,
    loss_ref, qg_ref, pg_ref, bg_ref,
    q4, bcol, pz, pb32, pz32, p32, pall,
    selt, idt, id_recv, smat, qs_send, qs_recv, pk_send, pk_recv,
    spart, sc1, sc2_send, sc2_recv, ss_all, st_all, w_all, lt_all, cf, cf_recv,
    yg_send, yg_recv, zp_part, zp_leaf, zp_chain, bk_part, bk_leaf, bk_chain, qx_send, qx_recv,
    q_s, q_r, pm_sem, bg_s, bg_r, pg_s, pg_r, qs_s, qs_r, id_s, id_r, pk_s, pk_r, cf_s, cf_r,
    sc_s, sc_r, ss_s, ss_r, st_s, st_r, w_s, w_r, lt_s, lt_r, yg_sem,
    br_s, br_r, pr_s, pr_r, qx_s, qx_r,
):
    dp = lax.axis_index("dp")
    j = lax.axis_index("sub")
    z = lax.div(dp, NC)
    c = lax.rem(dp, NC)
    x = lax.div(c, 2)
    yl = lax.rem(c, 2)
    yh = lax.div(j, 2)
    core = lax.rem(j, 2)

    def along(d):
        return lax.rem(z + NZ + d, NZ) * NC + c

    mate = dp + 1 - 2 * yl
    plane_c = [lax.rem(c + d, NC) for d in range(1, NC)]
    plane = [z * NC + v for v in plane_c]
    xs = [lax.rem(x + d, 4) for d in range(1, 4)]
    xdp = [z * NC + v * 2 + yl for v in xs]
    subs = [j + 1 - 2 * core, j + 2 - 4 * yh, 3 - j]

    barrier = pltpu.get_barrier_semaphore()
    for to_dp in (along(1), along(-1), along(2), along(-2), *plane):
        pl.semaphore_signal(barrier, inc=1, device_id=(to_dp, j), device_id_type=MESH)
    for to_sub in subs:
        pl.semaphore_signal(barrier, inc=1, device_id=(dp, to_sub), device_id_type=MESH)

    sent = []

    def go(src, dst, ssem, rsem, to_dp, to_sub):
        copy = pltpu.make_async_remote_copy(
            src_ref=src, dst_ref=dst, send_sem=ssem, recv_sem=rsem,
            device_id=(to_dp, to_sub), device_id_type=MESH,
        )
        copy.start()
        sent.append(copy)
        return copy

    p_own = p_ref[...].astype(F32)
    for k in range(8):
        pb32[k * 6 : k * 6 + 6, :] = p_own[:, k * 128 : (k + 1) * 128]
    pz[0, yl] = pb32[...].astype(BF16)
    bcol[0] = b_ref[...]
    q4[x] = q_ref[...]

    row = iota((128, 128), 0)
    lane = iota((128, 128), 1)
    eye = lane == row

    def col_to_row(v):
        return jnp.sum(jnp.where(eye, v, 0.0), 0, keepdims=True)

    def row_to_col(v):
        return jnp.sum(jnp.where(eye, v, 0.0), 1, keepdims=True)

    ids = ids_ref[...]
    owner = lax.shift_right_arithmetic(ids, 4)
    place = jnp.where(
        ids >= 0, (owner & 7) * 16 + lax.shift_right_arithmetic(owner, 3), -1
    )
    local = (ids & 15).astype(F32)
    many = jnp.zeros((128, 128), F32)
    w_sum = jnp.zeros((128, 128), F32)
    w_max = jnp.full((128, 128), -1.0, F32)
    for k in range(16):
        hit = place[k : k + 1, :] == row
        w_k = local[k : k + 1, :]
        many = many + jnp.where(hit, 1.0, 0.0)
        w_sum = w_sum + jnp.where(hit, w_k, 0.0)
        w_max = jnp.maximum(w_max, jnp.where(hit, w_k, -1.0))
    earlier = jnp.where(row < lane, 1.0, 0.0).astype(BF16)
    before = dot(many.astype(BF16), earlier, 1, 0)
    twice = (many > 1.5) & (before < 0.5)
    first = (many > 0.5) & (before < 0.5)
    second = ((many > 0.5) & (before > 0.5)) | twice
    w_second = jnp.where(twice, w_sum - w_max, w_max)
    id0 = jnp.sum(jnp.where(first, w_max + 1.0, 0.0), 1, keepdims=True) - 1.0
    id1 = jnp.sum(jnp.where(second, w_second + 1.0, 0.0), 1, keepdims=True) - 1.0
    selt[0] = jnp.where(first, 1.0, 0.0)
    selt[1] = jnp.where(second, 1.0, 0.0)
    tile_row = iota((8, 128), 0)
    idt[...] = jnp.where(tile_row == 0, col_to_row(id0), col_to_row(id1))
    id_recv[c] = idt[...]
    for r in range(2):
        picked_q = dot(selt[r].astype(BF16), q_ref[...], 1, 0).astype(BF16)
        for k in range(NC):
            qs_send[k, r * 16 : (r + 1) * 16, :] = picked_q[k * 16 : (k + 1) * 16]
    qs_recv[c] = qs_send[c]

    pl.semaphore_wait(barrier, 14)

    def gather_stage(s, buf, ssem, rsem, log):
        if s > 0:
            for copy in log[s - 1]:
                copy.wait_recv()
        if s == 4:
            return
        up = (NZ - 2 * s) % NZ
        got = [
            go(buf.at[up], buf.at[14 - 2 * s], ssem.at[4 * s], rsem.at[4 * s], along(2), j),
            go(buf.at[up], buf.at[15 - 2 * s], ssem.at[4 * s + 1], rsem.at[4 * s + 1], along(1), j),
            go(buf.at[2 * s], buf.at[2 * s + 1], ssem.at[4 * s + 2], rsem.at[4 * s + 2], along(-1), j),
        ]
        if s < 3:
            got.append(go(buf.at[2 * s], buf.at[2 * s + 2], ssem.at[4 * s + 3], rsem.at[4 * s + 3], along(-2), j))
        log.append(got)

    p_log, b_log = [], []
    pm_copy = go(pz.at[0, yl], pz.at[0, yl], pm_sem.at[0], pm_sem.at[1], mate, j)
    gather_stage(0, bcol, bg_s, bg_r, b_log)
    id_copies = [go(idt, id_recv.at[c], id_s.at[d], id_r.at[d], plane[d], j) for d in range(7)]
    q_copies = [go(q_ref, q4.at[x], q_s.at[d], q_r.at[d], xdp[d], j) for d in range(3)]
    pm_copy.wait_recv()
    gather_stage(0, pz, pg_s, pg_r, p_log)

    def spread(k):
        pz32[...] = pz[k].reshape(96, 128).astype(F32)
        for y in range(2):
            for b in range(8):
                at = y * 48 + b * 6
                to = y * 96 + k * 6
                p32[to : to + 6, b * 128 : (b + 1) * 128] = pz32[at : at + 6, :]

    spread(0)
    gather_stage(1, bcol, bg_s, bg_r, b_log)
    gather_stage(1, pz, pg_s, pg_r, p_log)
    for k in (15, 14, 1, 2):
        spread(k)
    qs_copies = [go(qs_send.at[plane_c[d]], qs_recv.at[c], qs_s.at[d], qs_r.at[d], plane[d], j) for d in range(7)]
    gather_stage(2, bcol, bg_s, bg_r, b_log)
    gather_stage(2, pz, pg_s, pg_r, p_log)
    for k in (13, 12, 3, 4):
        spread(k)

    for copy in id_copies:
        copy.wait_recv()
    mine = iota((16, 128), 1) == c * 16 + iota((16, 128), 0)

    def to_column(tile_rows):
        return jnp.sum(jnp.where(mine, tile_rows, 0.0), 1, keepdims=True)

    offset = iota((16, 256), 0) - z
    offset = jnp.where(offset < 0, offset + NZ, offset)
    bank_lane = (iota((16, 256), 1) - offset * 16).astype(F32)
    for k in range(NC):
        for r in range(2):
            w_col = to_column(id_recv[k, r : r + 1, :])
            hot = (bank_lane == w_col) & (w_col > -0.5)
            at = k * 32 + r * 16
            smat[at : at + 16, :] = jnp.where(hot, 1.0, 0.0)

    gather_stage(3, bcol, bg_s, bg_r, b_log)
    gather_stage(3, pz, pg_s, pg_r, p_log)
    for k in (11, 10, 5, 6):
        spread(k)
    gather_stage(4, bcol, bg_s, bg_r, b_log)
    picked_b = dot(smat[...].astype(BF16), bcol[...].reshape(256, 1024), 1, 0)
    pk_send[...] = picked_b.astype(BF16).reshape(NC, 32, 1024)
    pk_copies = [go(pk_send.at[plane_c[d]], pk_recv.at[c], pk_s.at[d], pk_r.at[d], plane[d], j) for d in range(7)]
    pk_recv[c] = pk_send[c]
    gather_stage(4, pz, pg_s, pg_r, p_log)
    for k in (9, 8, 7):
        spread(k)
    pall[...] = p32[...].astype(BF16)

    for copy in q_copies:
        copy.wait_recv()
    for b in range(4):
        spart[b] = dot(pall[...], q4[b], 1, 1)
    sc_copies = [go(spart.at[1 - core + 2 * h], sc1.at[h], sc_s.at[h], sc_r.at[h], dp, subs[0]) for h in range(2)]
    for copy in sc_copies:
        copy.wait_recv()
    sc2_send[...] = spart[core + 2 - 2 * yh] + sc1[1 - yh]
    sc2_copy = go(sc2_send, sc2_recv, sc_s.at[2], sc_r.at[2], dp, subs[1])

    for copy in pk_copies:
        copy.wait_recv()

    def slots(ref, r):
        return ref[:, r * 16 : (r + 1) * 16, :].reshape(128, 1024)

    rows = []
    for r in range(2):
        prod = slots(qs_send, r).astype(F32) * slots(pk_recv, r).astype(F32)
        rows.append(col_to_row(jnp.sum(prod, 1, keepdims=True)))
    ss_all[j] = jnp.where(tile_row == 0, rows[0], rows[1])
    ss_copies = [go(ss_all.at[j], ss_all.at[j], ss_s.at[d], ss_r.at[d], dp, subs[d]) for d in range(3)]
    inv_row = 1.0 / cnt_ref[...].astype(F32)
    has = [selt[r] > 0.5 for r in range(2)]
    live = [jnp.sum(selt[r], 1, keepdims=True) > 0.5 for r in range(2)]
    inv_slot = [jnp.sum(jnp.where(has[r], inv_row, 0.0), 1, keepdims=True) for r in range(2)]
    for copy in ss_copies:
        copy.wait_recv()
    ss_rows = (((ss_all[0] + ss_all[1]) + ss_all[2]) + ss_all[3]) * SCALE
    ss = [row_to_col(ss_rows[r : r + 1]) for r in range(2)]
    low = [jnp.where(has[r], ss[r], -jnp.inf) for r in range(2)]
    p_max = jnp.max(jnp.maximum(low[0], low[1]), 0, keepdims=True)
    p_exp = jnp.sum(jnp.exp(low[0] - p_max) + jnp.exp(low[1] - p_max), 0, keepdims=True)
    p_sum = jnp.sum(
        jnp.where(has[0], ss[0], 0.0) + jnp.where(has[1], ss[1], 0.0), 0, keepdims=True
    )

    sc2_copy.wait_recv()
    scores = (spart[j] + sc1[yh] + sc2_recv[...]) * SCALE
    m_own = jnp.max(scores, 0, keepdims=True)
    here = x == j
    p_top = jnp.where(here, p_max, m_own)
    p_tot = jnp.where(here, p_exp, 0.0)
    m_all = jnp.maximum(m_own, p_top)
    s_all = jnp.sum(jnp.exp(scores - m_all), 0, keepdims=True)
    s_all = s_all + p_tot * jnp.exp(p_top - m_all)
    st_all[x] = jnp.where(tile_row == 0, m_all, s_all)
    st_copies = [go(st_all.at[x], st_all.at[x], st_s.at[d], st_r.at[d], xdp[d], j) for d in range(3)]
    for copy in st_copies:
        copy.wait_recv()
    tops = [st_all[b, 0:1, :] for b in range(4)]
    m_top = jnp.maximum(jnp.maximum(tops[0], tops[1]), jnp.maximum(tops[2], tops[3]))
    total = st_all[0, 1:2, :] * jnp.exp(tops[0] - m_top)
    for b in range(1, 4):
        total = total + st_all[b, 1:2, :] * jnp.exp(tops[b] - m_top)
    log_total = m_top + jnp.log(total)
    lt_all[j] = jnp.broadcast_to(log_total, (8, 128))
    w_all[j] = jnp.exp(scores - log_total).astype(BF16)
    w_far = go(w_all.at[j], w_all.at[j], w_s.at[1], w_r.at[1], dp, subs[1])
    w_near = go(w_all.at[j], w_all.at[j], w_s.at[0], w_r.at[0], dp, subs[0])
    lt_copies = [go(lt_all.at[j], lt_all.at[j], lt_s.at[d], lt_r.at[d], dp, subs[d]) for d in range(3)]

    for copy in lt_copies:
        copy.wait_recv()
    lt_row = lt_all[x, 0:1, :]
    coef = []
    for r in range(2):
        lt_slot = jnp.sum(jnp.where(has[r], lt_row, 0.0), 1, keepdims=True)
        weight = jnp.exp(jnp.where(live[r], ss[r] - lt_slot, 0.0))
        coef.append(jnp.where(live[r], weight - inv_slot[r], 0.0))
    cf[...] = jnp.where(tile_row == 0, col_to_row(coef[0]), col_to_row(coef[1]))
    cf_copies = [go(cf, cf_recv.at[c], cf_s.at[d], cf_r.at[d], plane[d], j) for d in range(7)]
    cf_recv[c] = cf[...]
    loss_ref[...] = lt_row - p_sum * inv_row

    w_far.wait_recv()
    far = core + 2 - 2 * yh
    w_pass = go(w_all.at[far], w_all.at[far], w_s.at[2], w_r.at[2], dp, subs[0])
    w_near.wait_recv()
    w_pass.wait_recv()

    def passage_part(y):
        at = pl.multiple_of(y * 96, 96)
        acc = dot(w_all[0, pl.ds(at, 96), :], q4[0], 1, 0)
        for b in range(1, 4):
            acc = acc + dot(w_all[b, pl.ds(at, 96), :], q4[b], 1, 0)
        return acc

    yg_send[...] = passage_part(1 - yl)
    yg_copy = go(yg_send, yg_recv, yg_sem.at[0], yg_sem.at[1], mate, j)

    for copy in cf_copies:
        copy.wait_recv()
    cols = []
    for k in range(NC):
        for r in range(2):
            cols.append(to_column(cf_recv[k, r : r + 1, :]))
    hi, lo = split(smat[...] * jnp.concatenate(cols, 0))
    for copy in qs_copies:
        copy.wait_recv()
    asked = qs_recv[...].reshape(256, 1024)
    bk_part[...] = (dot(hi, asked, 0, 0) + dot(lo, asked, 0, 0)).reshape(NZ, 16, 1024)

    def leaf(i, side, part_ref, leaf_ref, ssem, rsem, log):
        k, n, to = (2 * i + 1, i, along(1)) if side == 0 else (15 - 2 * i, 4 + i, along(-1))
        log[n] = go(part_ref.at[k], leaf_ref.at[side, i], ssem.at[n], rsem.at[n], to, j)

    def chain(s, side, part_ref, leaf_ref, chain_ref, ssem, rsem, log):
        k = 8 - 2 * s if side == 0 else 8 + 2 * s
        n = 8 + 4 * side + s
        if s > (0 if side == 0 else 1):
            log[n - 1].wait_recv()
            part_ref[k] += chain_ref[side, s - 1]
        if s > 0:
            log[4 * side + 4 - s].wait_recv()
            part_ref[k] += leaf_ref[side, 4 - s]
        log[n] = go(part_ref.at[k], chain_ref.at[side, s], ssem.at[n], rsem.at[n], along(2 - 4 * side), j)

    b_args = (bk_part, bk_leaf)
    p_args = (zp_part, zp_leaf)
    b_end, p_end = (br_s, br_r, {}), (pr_s, pr_r, {})

    def start_sums(a, ch, e):
        leaf(3, 0, *a, *e)
        leaf(3, 1, *a, *e)
        chain(0, 0, *a, ch, *e)
        for i in (2, 1, 0):
            leaf(i, 0, *a, *e)
            leaf(i, 1, *a, *e)

    def sums_stage(s, a, ch, e):
        chain(s, 0, *a, ch, *e)
        chain(s, 1, *a, ch, *e)

    def sums_end(a, ch, e):
        log = e[2]
        for n in (0, 4, 11, 15):
            log[n].wait_recv()
        return a[0][0] + a[1][0, 0] + a[1][1, 0] + ch[0, 3] + ch[1, 3]

    start_sums(b_args, bk_chain, b_end)

    p32[0:96, :] = passage_part(yl)
    p_half = pall[...]
    qx_copies = []
    for d in range(3):
        qx_send[d] = dot(w_all[xs[d]], p_half, 0, 0).astype(BF16)
        qx_copies.append(go(qx_send.at[d], qx_recv.at[d], qx_s.at[d], qx_r.at[d], xdp[d], j))
    sums_stage(1, b_args, bk_chain, b_end)
    zp_part[...] = jnp.zeros((NZ, 8, 1024), F32)
    yg_copy.wait_recv()
    p32[0:96, :] = p32[0:96, :] + yg_recv[...]
    for k in range(NZ):
        zp_part[k, 0:6, :] = p32[k * 6 : k * 6 + 6, :]
    start_sums(p_args, zp_chain, p_end)

    mine_g = dot(w_all[x], p_half, 0, 0)
    for r in range(2):
        hi, lo = split(selt[r] * coef[r])
        rows_b = slots(pk_recv, r)
        mine_g = mine_g + dot(hi, rows_b, 0, 0) + dot(lo, rows_b, 0, 0)
    qg_ref[...] = mine_g
    sums_stage(2, b_args, bk_chain, b_end)
    sums_stage(1, p_args, zp_chain, p_end)
    sums_stage(3, b_args, bk_chain, b_end)
    sums_stage(2, p_args, zp_chain, p_end)
    for copy in qx_copies:
        copy.wait_recv()
    others = qx_recv[0].astype(F32) + qx_recv[1].astype(F32) + qx_recv[2].astype(F32)
    qg_ref[...] = SCALE * (qg_ref[...] + others)
    sums_stage(3, p_args, zp_chain, p_end)
    bg_ref[...] = SCALE * sums_end(b_args, bk_chain, b_end)
    pg_ref[...] = SCALE * sums_end(p_args, zp_chain, p_end)[0:6]
    for copy in sent:
        copy.wait_send()


def body(queries, passages, positive_bank, positive_ids, positive_counts):
    vmem = pl.BlockSpec(memory_space=pltpu.VMEM)
    dma = pltpu.SemaphoreType.DMA

    def buf(*shape):
        return pltpu.VMEM(shape, F32)

    def buf16(*shape):
        return pltpu.VMEM(shape, BF16)

    def sems(*counts):
        return [dma((n,)) for n in counts]

    scratch = [
        buf16(4, 128, 1024), buf16(NZ, 16, 1024), buf16(NZ, 2, 48, 128), buf(48, 128), buf(96, 128),
        buf(192, 1024), buf16(192, 1024),
        buf(2, 128, 128), buf(8, 128), buf(NC, 8, 128), buf(256, 256), buf16(NC, 32, 1024),
        buf16(NC, 32, 1024), buf16(NC, 32, 1024), buf16(NC, 32, 1024),
        buf(4, 192, 128), buf(2, 192, 128), buf(192, 128), buf(192, 128), buf(4, 8, 128), buf(4, 8, 128),
        buf16(4, 192, 128), buf(4, 8, 128), buf(8, 128), buf(NC, 8, 128),
        buf(96, 1024), buf(96, 1024), buf(NZ, 8, 1024), buf(2, 4, 8, 1024), buf(2, 4, 8, 1024),
        buf(NZ, 16, 1024), buf(2, 4, 16, 1024), buf(2, 4, 16, 1024), buf16(3, 128, 1024), buf16(3, 128, 1024),
        *sems(3, 3, 2, 16, 16, 16, 16, 7, 7, 7, 7, 7, 7, 7, 7),
        *sems(3, 3, 3, 3, 3, 3, 3, 3, 3, 3, 2),
        *sems(16, 16, 16, 16, 3, 3),
    ]
    losses, query_grad, passage_grad, bank_grad = pl.pallas_call(
        kernel,
        out_shape=(
            jax.ShapeDtypeStruct((1, 128), F32),
            jax.ShapeDtypeStruct((128, 1024), F32),
            jax.ShapeDtypeStruct((6, 1024), F32),
            jax.ShapeDtypeStruct((16, 1024), F32),
        ),
        in_specs=[vmem] * 5,
        out_specs=(vmem,) * 4,
        scratch_shapes=scratch,
        compiler_params=pltpu.CompilerParams(
            collective_id=0, has_side_effects=True, vmem_limit_bytes=48 * 2**20
        ),
    )(queries, passages, positive_bank, positive_ids.T, positive_counts.reshape(1, -1))
    return losses.reshape(-1), query_grad, passage_grad, bank_grad


def solution(mesh):
    placed = (P("dp", "sub"), P("dp", "sub"), P("dp", "sub"), P("dp", None), P("dp"))
    return jax.shard_map(
        body,
        mesh=mesh,
        in_specs=placed,
        out_specs=(P("dp"), P("dp", "sub"), P("dp", "sub"), P("dp", "sub")),
        check_vma=False,
    )
```

time: 124 us -> 95.8 us (0.77)
  the two profiles are of different devices: /device:TPU:14 before, /device:TPU:32 now
where the time goes in v2:
time: 95.8 us; the launch traced here: 95.5 us
  Pallas kernels  88.5 us (92%)
  local copies, waits for them, and re-layouts  6.32 us (7%)
    pallas_call x1, Pallas kernels, body(): pl.pallas_call(kernel, out_shape=(jax.ShapeDtypeStruct((1, 128), F32), ja...  88.5 us
    unnamed x14, local copies, waits for them, and re-layouts  6.32 us

profile of v2, /device:TPU:32, one launch (start us, length us, event | category | flops | bytes accessed | tf_op | source)
XLA Modules:
  0.0 95.5 jit_solution(13571016639123051305)
XLA Ops:
  0.6 0.0 copy-start.4
  0.6 0.6 copy-done.4
  1.3 0.0 copy-start
  1.3 0.9 copy-done
  2.2 0.0 copy-start.1
  2.2 0.8 copy-done.1
  3.0 0.0 copy-start.2
  3.0 0.7 copy-done.2
  3.7 0.0 copy-start.3
  3.7 0.7 copy-done.3
  4.4 88.5 %shard_map.84 = (f32[1,128]{1,0:T(1,128)S(1)}, f32[128,1024]{1,0:T(8,128)S(1)}, f32[6,1024]{1,0:T(8,128)S(1)}, f32[16,1024]{1,0:T(8,128)S(1)}) custom-call(bf16[128,1024]{1,0:T(8,128)(2,1)S(1)} %copy-done, bf16[6,1024]{1,0:T(8,128)(2,1)S(1)} %copy-done.2, bf16[16,1024]{1,0:T(8,128)(2,1)S(1)} %copy-done.1, s32[16,128]{1,0:T(8,128)S(1)} %bitcast.3, ...), custom_call_target="tpu_custom_call" | custom-call | tf_op jit(solution)/shard_map/pallas_call | solution.py:406
  93.0 0.5 copy.13
  93.5 0.8 copy.14
  94.3 0.6 copy.15
  94.9 0.6 copy.16
Async XLA Ops:
  0.6 0.7 copy-start.4
  1.3 0.9 copy-start
  2.2 0.8 copy-start.1
  3.0 0.7 copy-start.2
  3.7 0.7 copy-start.3

commit v3 on v2

--- a/solution.py
+++ b/solution.py
@@ -11,6 +11,7 @@
 NZ = 16
 NC = 8
 SCALE = 50.0
+FAR_FIRST = (8, 7, 9, 6, 10, 5, 11, 4, 12, 3, 13, 2, 14, 1, 15)
 
 
 def iota(shape, dim):
@@ -32,10 +33,10 @@
     q4, bcol, pz, pb32, pz32, p32, pall,
     selt, idt, id_recv, smat, qs_send, qs_recv, pk_send, pk_recv,
     spart, sc1, sc2_send, sc2_recv, ss_all, st_all, w_all, lt_all, cf, cf_recv,
-    yg_send, yg_recv, zp_part, zp_leaf, zp_chain, bk_part, bk_leaf, bk_chain, qx_send, qx_recv,
+    yg_send, yg_recv, zp_part, zp_leaf, zp_chain, aq_send, aq_recv, vid, vcf, cz_send, cz_recv, qx_send, qx_recv,
     q_s, q_r, pm_sem, bg_s, bg_r, pg_s, pg_r, qs_s, qs_r, id_s, id_r, pk_s, pk_r, cf_s, cf_r,
-    sc_s, sc_r, ss_s, ss_r, st_s, st_r, w_s, w_r, lt_s, lt_r, yg_sem,
-    br_s, br_r, pr_s, pr_r, qx_s, qx_r,
+    sc_s, sc_r, ss_s, ss_r, st_s, st_r, w_s, w_r, lt_s, lt_r, yg_s, yg_r,
+    aq_s, aq_r, cz_s, cz_r, pr_s, pr_r, qx_s, qx_r,
 ):
     dp = lax.axis_index("dp")
     j = lax.axis_index("sub")
@@ -159,13 +160,13 @@
                 p32[to : to + 6, b * 128 : (b + 1) * 128] = pz32[at : at + 6, :]
 
     spread(0)
+    gather_stage(1, pz, pg_s, pg_r, p_log)
     gather_stage(1, bcol, bg_s, bg_r, b_log)
-    gather_stage(1, pz, pg_s, pg_r, p_log)
     for k in (15, 14, 1, 2):
         spread(k)
     qs_copies = [go(qs_send.at[plane_c[d]], qs_recv.at[c], qs_s.at[d], qs_r.at[d], plane[d], j) for d in range(7)]
+    gather_stage(2, pz, pg_s, pg_r, p_log)
     gather_stage(2, bcol, bg_s, bg_r, b_log)
-    gather_stage(2, pz, pg_s, pg_r, p_log)
     for k in (13, 12, 3, 4):
         spread(k)
 
@@ -179,22 +180,21 @@
     offset = iota((16, 256), 0) - z
     offset = jnp.where(offset < 0, offset + NZ, offset)
     bank_lane = (iota((16, 256), 1) - offset * 16).astype(F32)
+    slot_lane = iota((16, 128), 1) & 15
+    ids_by = jnp.zeros((16, 128), F32)
     for k in range(NC):
         for r in range(2):
             w_col = to_column(id_recv[k, r : r + 1, :])
             hot = (bank_lane == w_col) & (w_col > -0.5)
             at = k * 32 + r * 16
-            smat[at : at + 16, :] = jnp.where(hot, 1.0, 0.0)
-
+            smat[at : at + 16, :] = jnp.where(hot, 1.0, 0.0).astype(BF16)
+            ids_by = jnp.where(slot_lane == k * 2 + r, w_col + 1.0, ids_by)
+    vid[...] = ids_by
+
+    gather_stage(3, pz, pg_s, pg_r, p_log)
     gather_stage(3, bcol, bg_s, bg_r, b_log)
-    gather_stage(3, pz, pg_s, pg_r, p_log)
     for k in (11, 10, 5, 6):
         spread(k)
-    gather_stage(4, bcol, bg_s, bg_r, b_log)
-    picked_b = dot(smat[...].astype(BF16), bcol[...].reshape(256, 1024), 1, 0)
-    pk_send[...] = picked_b.astype(BF16).reshape(NC, 32, 1024)
-    pk_copies = [go(pk_send.at[plane_c[d]], pk_recv.at[c], pk_s.at[d], pk_r.at[d], plane[d], j) for d in range(7)]
-    pk_recv[c] = pk_send[c]
     gather_stage(4, pz, pg_s, pg_r, p_log)
     for k in (9, 8, 7):
         spread(k)
@@ -202,13 +202,37 @@
 
     for copy in q_copies:
         copy.wait_recv()
-    for b in range(4):
+    sc_copies = []
+    for h in range(2):
+        b = 1 - core + 2 * h
         spart[b] = dot(pall[...], q4[b], 1, 1)
-    sc_copies = [go(spart.at[1 - core + 2 * h], sc1.at[h], sc_s.at[h], sc_r.at[h], dp, subs[0]) for h in range(2)]
+        sc_copies.append(go(spart.at[b], sc1.at[h], sc_s.at[h], sc_r.at[h], dp, subs[0]))
+    for h in range(2):
+        b = core + 2 * h
+        spart[b] = dot(pall[...], q4[b], 1, 1)
+
+    gather_stage(4, bcol, bg_s, bg_r, b_log)
+    picked_b = dot(smat[...], bcol[...].reshape(256, 1024), 1, 0)
+    pk_send[...] = picked_b.astype(BF16).reshape(NC, 32, 1024)
+    pk_copies = [go(pk_send.at[plane_c[d]], pk_recv.at[c], pk_s.at[d], pk_r.at[d], plane[d], j) for d in range(7)]
+    pk_recv[c] = pk_send[c]
+
     for copy in sc_copies:
         copy.wait_recv()
     sc2_send[...] = spart[core + 2 - 2 * yh] + sc1[1 - yh]
     sc2_copy = go(sc2_send, sc2_recv, sc_s.at[2], sc_r.at[2], dp, subs[1])
+
+    for copy in qs_copies:
+        copy.wait_recv()
+    goal = iota((256, 256), 0)
+    plane_of = z + lax.shift_right_logical(goal, 4)
+    plane_of = jnp.where(plane_of >= NZ, plane_of - NZ, plane_of)
+    goal = (lax.shift_right_logical(goal, 1) & 7) * 32 + (goal & 1) * 16 + plane_of
+    order = jnp.where(iota((256, 256), 1) == goal, 1.0, 0.0).astype(BF16)
+    by_plane = dot(order, qs_recv[...].reshape(256, 1024), 1, 0)
+    aq_send[...] = by_plane.astype(BF16).reshape(NZ, 16, 1024)
+    aq_recv[0] = aq_send[0]
+    aq_copies = [go(aq_send.at[k], aq_recv.at[NZ - k], aq_s.at[k - 1], aq_r.at[NZ - k - 1], along(k), j) for k in FAR_FIRST]
 
     for copy in pk_copies:
         copy.wait_recv()
@@ -289,19 +313,28 @@
         return acc
 
     yg_send[...] = passage_part(1 - yl)
-    yg_copy = go(yg_send, yg_recv, yg_sem.at[0], yg_sem.at[1], mate, j)
+    yg_copies = []
+    for n, (at, size) in enumerate(((24, 48), (0, 24), (72, 24))):
+        piece = pl.ds(at, size)
+        yg_copies.append(go(yg_send.at[piece], yg_recv.at[piece], yg_s.at[n], yg_r.at[n], mate, j))
 
     for copy in cf_copies:
         copy.wait_recv()
-    cols = []
+    cf_by = jnp.zeros((16, 128), F32)
     for k in range(NC):
         for r in range(2):
-            cols.append(to_column(cf_recv[k, r : r + 1, :]))
-    hi, lo = split(smat[...] * jnp.concatenate(cols, 0))
-    for copy in qs_copies:
-        copy.wait_recv()
-    asked = qs_recv[...].reshape(256, 1024)
-    bk_part[...] = (dot(hi, asked, 0, 0) + dot(lo, asked, 0, 0)).reshape(NZ, 16, 1024)
+            cf_by = jnp.where(slot_lane == k * 2 + r, to_column(cf_recv[k, r : r + 1, :]), cf_by)
+    vcf[...] = cf_by
+    tile_group = lax.shift_right_logical(iota((8, 128), 1), 4)
+    for k in range(NZ):
+        oz = lax.rem(z + k, NZ)
+        m = (NZ - k) % NZ
+        here_cf = (tile_row == m // 8) & (tile_group == m % 8)
+        here_id = (tile_row == m // 8 + 2) & (tile_group == m % 8)
+        tile = jnp.where(here_cf, vcf[pl.ds(oz, 1), :], 0.0)
+        cz_send[k] = jnp.where(here_id, vid[pl.ds(oz, 1), :], tile)
+    cz_recv[0] = cz_send[0]
+    cz_copies = [go(cz_send.at[k], cz_recv.at[NZ - k], cz_s.at[k - 1], cz_r.at[NZ - k - 1], along(k), j) for k in FAR_FIRST]
 
     def leaf(i, side, part_ref, leaf_ref, ssem, rsem, log):
         k, n, to = (2 * i + 1, i, along(1)) if side == 0 else (15 - 2 * i, 4 + i, along(-1))
@@ -318,43 +351,35 @@
             part_ref[k] += leaf_ref[side, 4 - s]
         log[n] = go(part_ref.at[k], chain_ref.at[side, s], ssem.at[n], rsem.at[n], along(2 - 4 * side), j)
 
-    b_args = (bk_part, bk_leaf)
-    p_args = (zp_part, zp_leaf)
-    b_end, p_end = (br_s, br_r, {}), (pr_s, pr_r, {})
-
-    def start_sums(a, ch, e):
-        leaf(3, 0, *a, *e)
-        leaf(3, 1, *a, *e)
-        chain(0, 0, *a, ch, *e)
-        for i in (2, 1, 0):
-            leaf(i, 0, *a, *e)
-            leaf(i, 1, *a, *e)
-
-    def sums_stage(s, a, ch, e):
-        chain(s, 0, *a, ch, *e)
-        chain(s, 1, *a, ch, *e)
-
-    def sums_end(a, ch, e):
-        log = e[2]
-        for n in (0, 4, 11, 15):
-            log[n].wait_recv()
-        return a[0][0] + a[1][0, 0] + a[1][1, 0] + ch[0, 3] + ch[1, 3]
-
-    start_sums(b_args, bk_chain, b_end)
-
+    sums = (zp_part, zp_leaf)
+    ends = (pr_s, pr_r, {})
+
+    def sums_stage(s):
+        chain(s, 0, *sums, zp_chain, *ends)
+        if s > 0:
+            chain(s, 1, *sums, zp_chain, *ends)
+
+    def leaves(i):
+        leaf(i, 0, *sums, *ends)
+        leaf(i, 1, *sums, *ends)
+
+    def both_halves(k):
+        at = slice(k * 6, k * 6 + 6)
+        zp_part[k, 0:6, :] = p32[at, :] + yg_recv[at, :]
+
+    zp_part[...] = jnp.zeros((NZ, 8, 1024), F32)
     p32[0:96, :] = passage_part(yl)
     p_half = pall[...]
     qx_copies = []
     for d in range(3):
         qx_send[d] = dot(w_all[xs[d]], p_half, 0, 0).astype(BF16)
         qx_copies.append(go(qx_send.at[d], qx_recv.at[d], qx_s.at[d], qx_r.at[d], xdp[d], j))
-    sums_stage(1, b_args, bk_chain, b_end)
-    zp_part[...] = jnp.zeros((NZ, 8, 1024), F32)
-    yg_copy.wait_recv()
-    p32[0:96, :] = p32[0:96, :] + yg_recv[...]
-    for k in range(NZ):
-        zp_part[k, 0:6, :] = p32[k * 6 : k * 6 + 6, :]
-    start_sums(p_args, zp_chain, p_end)
+    yg_copies[0].wait_recv()
+    for k in range(4, 12):
+        both_halves(k)
+    leaves(3)
+    sums_stage(0)
+    leaves(2)
 
     mine_g = dot(w_all[x], p_half, 0, 0)
     for r in range(2):
@@ -362,17 +387,36 @@
         rows_b = slots(pk_recv, r)
         mine_g = mine_g + dot(hi, rows_b, 0, 0) + dot(lo, rows_b, 0, 0)
     qg_ref[...] = mine_g
-    sums_stage(2, b_args, bk_chain, b_end)
-    sums_stage(1, p_args, zp_chain, p_end)
-    sums_stage(3, b_args, bk_chain, b_end)
-    sums_stage(2, p_args, zp_chain, p_end)
+    sums_stage(1)
+    for copy in yg_copies[1:]:
+        copy.wait_recv()
+    for k in (0, 1, 2, 3, 12, 13, 14, 15):
+        both_halves(k)
+    leaves(1)
+    leaves(0)
+
+    for copy in cz_copies + aq_copies:
+        copy.wait_recv()
+    tiles = cz_recv[0]
+    for k in range(1, NZ):
+        tiles = tiles + cz_recv[k]
+    bank_sum = jnp.zeros((16, 1024), F32)
+    bank_row = (iota((16, 128), 0) + 1).astype(F32)
+    for h in range(2):
+        hi, lo = split(jnp.where(tiles[h + 2 : h + 3] == bank_row, tiles[h : h + 1], 0.0))
+        asked = aq_recv[8 * h : 8 * h + 8].reshape(128, 1024)
+        bank_sum = bank_sum + dot(hi, asked, 1, 0) + dot(lo, asked, 1, 0)
+    bg_ref[...] = SCALE * bank_sum
+    sums_stage(2)
     for copy in qx_copies:
         copy.wait_recv()
     others = qx_recv[0].astype(F32) + qx_recv[1].astype(F32) + qx_recv[2].astype(F32)
     qg_ref[...] = SCALE * (qg_ref[...] + others)
-    sums_stage(3, p_args, zp_chain, p_end)
-    bg_ref[...] = SCALE * sums_end(b_args, bk_chain, b_end)
-    pg_ref[...] = SCALE * sums_end(p_args, zp_chain, p_end)[0:6]
+    sums_stage(3)
+    for n in (0, 4, 11, 15):
+        ends[2][n].wait_recv()
+    total_p = zp_part[0] + zp_leaf[0, 0] + zp_leaf[1, 0] + zp_chain[0, 3] + zp_chain[1, 3]
+    pg_ref[...] = SCALE * total_p[0:6]
     for copy in sent:
         copy.wait_send()
 
@@ -393,15 +437,16 @@
     scratch = [
         buf16(4, 128, 1024), buf16(NZ, 16, 1024), buf16(NZ, 2, 48, 128), buf(48, 128), buf(96, 128),
         buf(192, 1024), buf16(192, 1024),
-        buf(2, 128, 128), buf(8, 128), buf(NC, 8, 128), buf(256, 256), buf16(NC, 32, 1024),
+        buf(2, 128, 128), buf(8, 128), buf(NC, 8, 128), buf16(256, 256), buf16(NC, 32, 1024),
         buf16(NC, 32, 1024), buf16(NC, 32, 1024), buf16(NC, 32, 1024),
         buf(4, 192, 128), buf(2, 192, 128), buf(192, 128), buf(192, 128), buf(4, 8, 128), buf(4, 8, 128),
         buf16(4, 192, 128), buf(4, 8, 128), buf(8, 128), buf(NC, 8, 128),
         buf(96, 1024), buf(96, 1024), buf(NZ, 8, 1024), buf(2, 4, 8, 1024), buf(2, 4, 8, 1024),
-        buf(NZ, 16, 1024), buf(2, 4, 16, 1024), buf(2, 4, 16, 1024), buf16(3, 128, 1024), buf16(3, 128, 1024),
+        buf16(NZ, 16, 1024), buf16(NZ, 16, 1024), buf(16, 128), buf(16, 128), buf(NZ, 8, 128), buf(NZ, 8, 128),
+        buf16(3, 128, 1024), buf16(3, 128, 1024),
         *sems(3, 3, 2, 16, 16, 16, 16, 7, 7, 7, 7, 7, 7, 7, 7),
-        *sems(3, 3, 3, 3, 3, 3, 3, 3, 3, 3, 2),
-        *sems(16, 16, 16, 16, 3, 3),
+        *sems(3, 3, 3, 3, 3, 3, 3, 3, 3, 3, 3, 3),
+        *sems(15, 15, 15, 15, 16, 16, 3, 3),
     ]
     losses, query_grad, passage_grad, bank_grad = pl.pallas_call(
         kernel,

time: 95.8 us -> 86.8 us (0.906)
  the two profiles are of different devices: /device:TPU:32 before, /device:TPU:16 now
where the time goes in v3:
time: 86.8 us; the launch traced here: 86.5 us
  Pallas kernels  79.5 us (92%)
  local copies, waits for them, and re-layouts  6.32 us (7%)
    pallas_call x1, Pallas kernels, body(): pl.pallas_call(kernel, out_shape=(jax.ShapeDtypeStruct((1, 128), F32), ja...  79.5 us
    unnamed x14, local copies, waits for them, and re-layouts  6.32 us

profile of v3, /device:TPU:16, one launch (start us, length us, event | category | flops | bytes accessed | tf_op | source)
XLA Modules:
  0.0 86.5 jit_solution(3618648738366043632)
XLA Ops:
  0.6 0.0 copy-start.4
  0.6 0.6 copy-done.4
  1.3 0.0 copy-start
  1.3 0.9 %copy-done = bf16[128,1024]{1,0:T(8,128)(2,1)S(1)} copy-done((bf16[128,1024]{1,0:T(8,128)(2,1)S(1)}, bf16[128,1024]{1,0:T(8,128)(2,1)}, u32[]{:S(2)}) %copy-start) | copy-done | bytes 262168
  2.2 0.0 copy-start.1
  2.2 0.8 copy-done.1
  3.0 0.0 copy-start.2
  3.0 0.7 copy-done.2
  3.7 0.0 copy-start.3
  3.7 0.7 copy-done.3
  4.4 79.5 %shard_map.84 = (f32[1,128]{1,0:T(1,128)S(1)}, f32[128,1024]{1,0:T(8,128)S(1)}, f32[6,1024]{1,0:T(8,128)S(1)}, f32[16,1024]{1,0:T(8,128)S(1)}) custom-call(bf16[128,1024]{1,0:T(8,128)(2,1)S(1)} %copy-done, bf16[6,1024]{1,0:T(8,128)(2,1)S(1)} %copy-done.2, bf16[16,1024]{1,0:T(8,128)(2,1)S(1)} %copy-done.1, s32[16,128]{1,0:T(8,128)S(1)} %bitcast.3, ...), custom_call_target="tpu_custom_call" | custom-call | tf_op jit(solution)/shard_map/pallas_call | solution.py:451
  83.9 0.5 copy.13
  84.4 0.8 copy.14
  85.2 0.6 copy.15
  85.8 0.6 copy.16
Async XLA Ops:
  0.6 0.7 copy-start.4
  1.3 0.9 %copy-start = (bf16[128,1024]{1,0:T(8,128)(2,1)S(1)}, bf16[128,1024]{1,0:T(8,128)(2,1)}, u32[]{:S(2)}) copy-start(bf16[128,1024]{1,0:T(8,128)(2,1)} %q_ref.1) | copy-start | bytes 786436
  2.2 0.8 copy-start.1
  3.0 0.7 copy-start.2
  3.7 0.7 copy-start.3

commit v4 on v3

--- a/solution.py
+++ b/solution.py
@@ -33,10 +33,10 @@
     q4, bcol, pz, pb32, pz32, p32, pall,
     selt, idt, id_recv, smat, qs_send, qs_recv, pk_send, pk_recv,
     spart, sc1, sc2_send, sc2_recv, ss_all, st_all, w_all, lt_all, cf, cf_recv,
-    yg_send, yg_recv, zp_part, zp_leaf, zp_chain, aq_send, aq_recv, vid, vcf, cz_send, cz_recv, qx_send, qx_recv,
+    yg_send, yg_recv, yg32, zp_part, zp_leaf, zp_chain, aq_send, aq_recv, vid, vcf, cz_send, cz_recv, qx_send, qx_recv,
     q_s, q_r, pm_sem, bg_s, bg_r, pg_s, pg_r, qs_s, qs_r, id_s, id_r, pk_s, pk_r, cf_s, cf_r,
     sc_s, sc_r, ss_s, ss_r, st_s, st_r, w_s, w_r, lt_s, lt_r, yg_s, yg_r,
-    aq_s, aq_r, cz_s, cz_r, pr_s, pr_r, qx_s, qx_r,
+    aq_s, aq_r, cz_s, cz_r, pr_s, pr_r, qx_s, qx_r, in_sem,
 ):
     dp = lax.axis_index("dp")
     j = lax.axis_index("sub")
@@ -74,12 +74,15 @@
         sent.append(copy)
         return copy
 
+    fetch_q = pltpu.make_async_copy(q_ref, q4.at[x], in_sem.at[0])
+    fetch_b = pltpu.make_async_copy(b_ref, bcol.at[0], in_sem.at[1])
+    fetch_q.start()
+    fetch_b.start()
+
     p_own = p_ref[...].astype(F32)
     for k in range(8):
         pb32[k * 6 : k * 6 + 6, :] = p_own[:, k * 128 : (k + 1) * 128]
     pz[0, yl] = pb32[...].astype(BF16)
-    bcol[0] = b_ref[...]
-    q4[x] = q_ref[...]
 
     row = iota((128, 128), 0)
     lane = iota((128, 128), 1)
@@ -119,8 +122,10 @@
     tile_row = iota((8, 128), 0)
     idt[...] = jnp.where(tile_row == 0, col_to_row(id0), col_to_row(id1))
     id_recv[c] = idt[...]
+    fetch_q.wait()
+    fetch_b.wait()
     for r in range(2):
-        picked_q = dot(selt[r].astype(BF16), q_ref[...], 1, 0).astype(BF16)
+        picked_q = dot(selt[r].astype(BF16), q4[x], 1, 0).astype(BF16)
         for k in range(NC):
             qs_send[k, r * 16 : (r + 1) * 16, :] = picked_q[k * 16 : (k + 1) * 16]
     qs_recv[c] = qs_send[c]
@@ -129,25 +134,34 @@
 
     def gather_stage(s, buf, ssem, rsem, log):
         if s > 0:
-            for copy in log[s - 1]:
-                copy.wait_recv()
+            log[s - 1][0].wait_recv()
+            if s < 4:
+                log[s - 1][3].wait_recv()
         if s == 4:
             return
         up = (NZ - 2 * s) % NZ
         got = [
             go(buf.at[up], buf.at[14 - 2 * s], ssem.at[4 * s], rsem.at[4 * s], along(2), j),
+        ]
+        far = None
+        if s < 3:
+            far = go(buf.at[2 * s], buf.at[2 * s + 2], ssem.at[4 * s + 3], rsem.at[4 * s + 3], along(-2), j)
+        got += [
             go(buf.at[up], buf.at[15 - 2 * s], ssem.at[4 * s + 1], rsem.at[4 * s + 1], along(1), j),
             go(buf.at[2 * s], buf.at[2 * s + 1], ssem.at[4 * s + 2], rsem.at[4 * s + 2], along(-1), j),
+            far,
         ]
-        if s < 3:
-            got.append(go(buf.at[2 * s], buf.at[2 * s + 2], ssem.at[4 * s + 3], rsem.at[4 * s + 3], along(-2), j))
         log.append(got)
+
+    def sides(s, log):
+        log[s][1].wait_recv()
+        log[s][2].wait_recv()
 
     p_log, b_log = [], []
     pm_copy = go(pz.at[0, yl], pz.at[0, yl], pm_sem.at[0], pm_sem.at[1], mate, j)
     gather_stage(0, bcol, bg_s, bg_r, b_log)
     id_copies = [go(idt, id_recv.at[c], id_s.at[d], id_r.at[d], plane[d], j) for d in range(7)]
-    q_copies = [go(q_ref, q4.at[x], q_s.at[d], q_r.at[d], xdp[d], j) for d in range(3)]
+    q_copies = [go(q4.at[x], q4.at[x], q_s.at[d], q_r.at[d], xdp[d], j) for d in range(3)]
     pm_copy.wait_recv()
     gather_stage(0, pz, pg_s, pg_r, p_log)
 
@@ -162,11 +176,13 @@
     spread(0)
     gather_stage(1, pz, pg_s, pg_r, p_log)
     gather_stage(1, bcol, bg_s, bg_r, b_log)
+    sides(0, p_log)
     for k in (15, 14, 1, 2):
         spread(k)
     qs_copies = [go(qs_send.at[plane_c[d]], qs_recv.at[c], qs_s.at[d], qs_r.at[d], plane[d], j) for d in range(7)]
     gather_stage(2, pz, pg_s, pg_r, p_log)
     gather_stage(2, bcol, bg_s, bg_r, b_log)
+    sides(1, p_log)
     for k in (13, 12, 3, 4):
         spread(k)
 
@@ -193,9 +209,11 @@
 
     gather_stage(3, pz, pg_s, pg_r, p_log)
     gather_stage(3, bcol, bg_s, bg_r, b_log)
+    sides(2, p_log)
     for k in (11, 10, 5, 6):
         spread(k)
     gather_stage(4, pz, pg_s, pg_r, p_log)
+    sides(3, p_log)
     for k in (9, 8, 7):
         spread(k)
     pall[...] = p32[...].astype(BF16)
@@ -212,6 +230,8 @@
         spart[b] = dot(pall[...], q4[b], 1, 1)
 
     gather_stage(4, bcol, bg_s, bg_r, b_log)
+    for n in range(4):
+        sides(n, b_log)
     picked_b = dot(smat[...], bcol[...].reshape(256, 1024), 1, 0)
     pk_send[...] = picked_b.astype(BF16).reshape(NC, 32, 1024)
     pk_copies = [go(pk_send.at[plane_c[d]], pk_recv.at[c], pk_s.at[d], pk_r.at[d], plane[d], j) for d in range(7)]
@@ -286,6 +306,9 @@
     w_near = go(w_all.at[j], w_all.at[j], w_s.at[0], w_r.at[0], dp, subs[0])
     lt_copies = [go(lt_all.at[j], lt_all.at[j], lt_s.at[d], lt_r.at[d], dp, subs[d]) for d in range(3)]
 
+    w_far.wait_recv()
+    far = core + 2 - 2 * yh
+    w_pass = go(w_all.at[far], w_all.at[far], w_s.at[2], w_r.at[2], dp, subs[0])
     for copy in lt_copies:
         copy.wait_recv()
     lt_row = lt_all[x, 0:1, :]
@@ -299,9 +322,6 @@
     cf_recv[c] = cf[...]
     loss_ref[...] = lt_row - p_sum * inv_row
 
-    w_far.wait_recv()
-    far = core + 2 - 2 * yh
-    w_pass = go(w_all.at[far], w_all.at[far], w_s.at[2], w_r.at[2], dp, subs[0])
     w_near.wait_recv()
     w_pass.wait_recv()
 
@@ -312,9 +332,9 @@
             acc = acc + dot(w_all[b, pl.ds(at, 96), :], q4[b], 1, 0)
         return acc
 
-    yg_send[...] = passage_part(1 - yl)
+    yg_send[...] = passage_part(1 - yl).astype(BF16)
     yg_copies = []
-    for n, (at, size) in enumerate(((24, 48), (0, 24), (72, 24))):
+    for n, (at, size) in enumerate(((16, 64), (0, 16), (80, 16))):
         piece = pl.ds(at, size)
         yg_copies.append(go(yg_send.at[piece], yg_recv.at[piece], yg_s.at[n], yg_r.at[n], mate, j))
 
@@ -365,7 +385,7 @@
 
     def both_halves(k):
         at = slice(k * 6, k * 6 + 6)
-        zp_part[k, 0:6, :] = p32[at, :] + yg_recv[at, :]
+        zp_part[k, 0:6, :] = p32[at, :] + yg32[at, :]
 
     zp_part[...] = jnp.zeros((NZ, 8, 1024), F32)
     p32[0:96, :] = passage_part(yl)
@@ -375,6 +395,7 @@
         qx_send[d] = dot(w_all[xs[d]], p_half, 0, 0).astype(BF16)
         qx_copies.append(go(qx_send.at[d], qx_recv.at[d], qx_s.at[d], qx_r.at[d], xdp[d], j))
     yg_copies[0].wait_recv()
+    yg32[16:80, :] = yg_recv[16:80, :].astype(F32)
     for k in range(4, 12):
         both_halves(k)
     leaves(3)
@@ -390,6 +411,8 @@
     sums_stage(1)
     for copy in yg_copies[1:]:
         copy.wait_recv()
+    yg32[0:16, :] = yg_recv[0:16, :].astype(F32)
+    yg32[80:96, :] = yg_recv[80:96, :].astype(F32)
     for k in (0, 1, 2, 3, 12, 13, 14, 15):
         both_halves(k)
     leaves(1)
@@ -423,6 +446,7 @@
 
 def body(queries, passages, positive_bank, positive_ids, positive_counts):
     vmem = pl.BlockSpec(memory_space=pltpu.VMEM)
+    hbm = pl.BlockSpec(memory_space=pl.ANY)
     dma = pltpu.SemaphoreType.DMA
 
     def buf(*shape):
@@ -441,12 +465,12 @@
         buf16(NC, 32, 1024), buf16(NC, 32, 1024), buf16(NC, 32, 1024),
         buf(4, 192, 128), buf(2, 192, 128), buf(192, 128), buf(192, 128), buf(4, 8, 128), buf(4, 8, 128),
         buf16(4, 192, 128), buf(4, 8, 128), buf(8, 128), buf(NC, 8, 128),
-        buf(96, 1024), buf(96, 1024), buf(NZ, 8, 1024), buf(2, 4, 8, 1024), buf(2, 4, 8, 1024),
+        buf16(96, 1024), buf16(96, 1024), buf(96, 1024), buf(NZ, 8, 1024), buf(2, 4, 8, 1024), buf(2, 4, 8, 1024),
         buf16(NZ, 16, 1024), buf16(NZ, 16, 1024), buf(16, 128), buf(16, 128), buf(NZ, 8, 128), buf(NZ, 8, 128),
         buf16(3, 128, 1024), buf16(3, 128, 1024),
         *sems(3, 3, 2, 16, 16, 16, 16, 7, 7, 7, 7, 7, 7, 7, 7),
         *sems(3, 3, 3, 3, 3, 3, 3, 3, 3, 3, 3, 3),
-        *sems(15, 15, 15, 15, 16, 16, 3, 3),
+        *sems(15, 15, 15, 15, 16, 16, 3, 3, 2),
     ]
     losses, query_grad, passage_grad, bank_grad = pl.pallas_call(
         kernel,
@@ -456,7 +480,7 @@
             jax.ShapeDtypeStruct((6, 1024), F32),
             jax.ShapeDtypeStruct((16, 1024), F32),
         ),
-        in_specs=[vmem] * 5,
+        in_specs=[hbm, vmem, hbm, vmem, vmem],
         out_specs=(vmem,) * 4,
         scratch_shapes=scratch,
         compiler_params=pltpu.CompilerParams(

time: 86.8 us -> 85.9 us (0.990)
  the two profiles are of different devices: /device:TPU:16 before, /device:TPU:56 now
where the time goes in v4:
time: 85.9 us; the launch traced here: 85.5 us
  Pallas kernels  78.6 us (92%)
  local copies, waits for them, and re-layouts  6.32 us (7%)
    pallas_call x1, Pallas kernels, body(): pl.pallas_call(kernel, out_shape=(jax.ShapeDtypeStruct((1, 128), F32), ja...  78.6 us
    unnamed x14, local copies, waits for them, and re-layouts  6.32 us

profile of v4, /device:TPU:56, one launch (start us, length us, event | category | flops | bytes accessed | tf_op | source)
XLA Modules:
  0.0 85.5 jit_solution(10112952031394147788)
XLA Ops:
  0.6 0.0 copy-start.4
  0.6 0.6 copy-done.4
  1.3 0.0 copy-start
  1.3 0.9 %copy-done = bf16[128,1024]{1,0:T(8,128)(2,1)S(1)} copy-done((bf16[128,1024]{1,0:T(8,128)(2,1)S(1)}, bf16[128,1024]{1,0:T(8,128)(2,1)}, u32[]{:S(2)}) %copy-start) | copy-done | bytes 262168
  2.2 0.0 copy-start.1
  2.2 0.8 copy-done.1
  3.0 0.0 copy-start.2
  3.0 0.7 copy-done.2
  3.7 0.0 copy-start.3
  3.7 0.7 copy-done.3
  4.4 78.6 %shard_map.84 = (f32[1,128]{1,0:T(1,128)S(1)}, f32[128,1024]{1,0:T(8,128)S(1)}, f32[6,1024]{1,0:T(8,128)S(1)}, f32[16,1024]{1,0:T(8,128)S(1)}) custom-call(bf16[128,1024]{1,0:T(8,128)(2,1)S(1)} %copy-done, bf16[6,1024]{1,0:T(8,128)(2,1)S(1)} %copy-done.2, bf16[16,1024]{1,0:T(8,128)(2,1)S(1)} %copy-done.1, s32[16,128]{1,0:T(8,128)S(1)} %bitcast.3, ...), custom_call_target="tpu_custom_call" | custom-call | tf_op jit(solution)/shard_map/pallas_call | solution.py:475
  83.0 0.5 copy.13
  83.5 0.8 copy.14
  84.3 0.6 copy.15
  84.9 0.6 copy.16
Async XLA Ops:
  0.6 0.7 copy-start.4
  1.3 0.9 %copy-start = (bf16[128,1024]{1,0:T(8,128)(2,1)S(1)}, bf16[128,1024]{1,0:T(8,128)(2,1)}, u32[]{:S(2)}) copy-start(bf16[128,1024]{1,0:T(8,128)(2,1)} %q_ref.1) | copy-start | bytes 786436
  2.2 0.8 copy-start.1
  3.0 0.7 copy-start.2
  3.7 0.7 copy-start.3

commit v5 on v4

--- a/solution.py
+++ b/solution.py
@@ -32,9 +32,9 @@
     loss_ref, qg_ref, pg_ref, bg_ref,
     q4, bcol, pz, pb32, pz32, p32, pall,
     selt, idt, id_recv, smat, qs_send, qs_recv, pk_send, pk_recv,
-    spart, sc1, sc2_send, sc2_recv, ss_all, st_all, w_all, lt_all, cf, cf_recv,
+    spart, sc1, sc2_send, sc2_recv, sl_send, sl_recv, ss_all, st_all, w_all, lt_all, cf, cf_recv,
     yg_send, yg_recv, yg32, zp_part, zp_leaf, zp_chain, aq_send, aq_recv, vid, vcf, cz_send, cz_recv, qx_send, qx_recv,
-    q_s, q_r, pm_sem, bg_s, bg_r, pg_s, pg_r, qs_s, qs_r, id_s, id_r, pk_s, pk_r, cf_s, cf_r,
+    q_s, q_r, pm_sem, bg_s, bg_r, pg_s, pg_r, sl_s, sl_r, qs_s, qs_r, id_s, id_r, pk_s, pk_r, cf_s, cf_r,
     sc_s, sc_r, ss_s, ss_r, st_s, st_r, w_s, w_r, lt_s, lt_r, yg_s, yg_r,
     aq_s, aq_r, cz_s, cz_r, pr_s, pr_r, qx_s, qx_r, in_sem,
 ):
@@ -229,21 +229,30 @@
         b = core + 2 * h
         spart[b] = dot(pall[...], q4[b], 1, 1)
 
+    for copy in sc_copies:
+        copy.wait_recv()
+    sc2_send[...] = spart[core + 2 - 2 * yh] + sc1[1 - yh]
+    sc2_copy = go(sc2_send, sc2_recv, sc_s.at[2], sc_r.at[2], dp, subs[1])
+
     gather_stage(4, bcol, bg_s, bg_r, b_log)
     for n in range(4):
         sides(n, b_log)
     picked_b = dot(smat[...], bcol[...].reshape(256, 1024), 1, 0)
     pk_send[...] = picked_b.astype(BF16).reshape(NC, 32, 1024)
+    for copy in qs_copies:
+        copy.wait_recv()
+    pair = jnp.sum(picked_b * qs_recv[...].reshape(256, 1024).astype(F32), 1, keepdims=True)
+    for k in range(NC):
+        two = []
+        for r in range(2):
+            at = k * 32 + r * 16
+            two.append(jnp.sum(jnp.where(mine, pair[at : at + 16], 0.0), 0, keepdims=True))
+        sl_send[k] = jnp.where(tile_row == 0, two[0], jnp.where(tile_row == 1, two[1], 0.0))
+    sl_recv[c] = sl_send[c]
+    sl_copies = [go(sl_send.at[plane_c[d]], sl_recv.at[c], sl_s.at[d], sl_r.at[d], plane[d], j) for d in range(7)]
     pk_copies = [go(pk_send.at[plane_c[d]], pk_recv.at[c], pk_s.at[d], pk_r.at[d], plane[d], j) for d in range(7)]
     pk_recv[c] = pk_send[c]
 
-    for copy in sc_copies:
-        copy.wait_recv()
-    sc2_send[...] = spart[core + 2 - 2 * yh] + sc1[1 - yh]
-    sc2_copy = go(sc2_send, sc2_recv, sc_s.at[2], sc_r.at[2], dp, subs[1])
-
-    for copy in qs_copies:
-        copy.wait_recv()
     goal = iota((256, 256), 0)
     plane_of = z + lax.shift_right_logical(goal, 4)
     plane_of = jnp.where(plane_of >= NZ, plane_of - NZ, plane_of)
@@ -254,17 +263,12 @@
     aq_recv[0] = aq_send[0]
     aq_copies = [go(aq_send.at[k], aq_recv.at[NZ - k], aq_s.at[k - 1], aq_r.at[NZ - k - 1], along(k), j) for k in FAR_FIRST]
 
-    for copy in pk_copies:
-        copy.wait_recv()
-
-    def slots(ref, r):
-        return ref[:, r * 16 : (r + 1) * 16, :].reshape(128, 1024)
-
-    rows = []
-    for r in range(2):
-        prod = slots(qs_send, r).astype(F32) * slots(pk_recv, r).astype(F32)
-        rows.append(col_to_row(jnp.sum(prod, 1, keepdims=True)))
-    ss_all[j] = jnp.where(tile_row == 0, rows[0], rows[1])
+    for copy in sl_copies:
+        copy.wait_recv()
+    slot_tile = sl_recv[0]
+    for k in range(1, NC):
+        slot_tile = slot_tile + sl_recv[k]
+    ss_all[j] = slot_tile
     ss_copies = [go(ss_all.at[j], ss_all.at[j], ss_s.at[d], ss_r.at[d], dp, subs[d]) for d in range(3)]
     inv_row = 1.0 / cnt_ref[...].astype(F32)
     has = [selt[r] > 0.5 for r in range(2)]
@@ -402,6 +406,12 @@
     sums_stage(0)
     leaves(2)
 
+    for copy in pk_copies:
+        copy.wait_recv()
+
+    def slots(ref, r):
+        return ref[:, r * 16 : (r + 1) * 16, :].reshape(128, 1024)
+
     mine_g = dot(w_all[x], p_half, 0, 0)
     for r in range(2):
         hi, lo = split(selt[r] * coef[r])
@@ -463,12 +473,12 @@
         buf(192, 1024), buf16(192, 1024),
         buf(2, 128, 128), buf(8, 128), buf(NC, 8, 128), buf16(256, 256), buf16(NC, 32, 1024),
         buf16(NC, 32, 1024), buf16(NC, 32, 1024), buf16(NC, 32, 1024),
-        buf(4, 192, 128), buf(2, 192, 128), buf(192, 128), buf(192, 128), buf(4, 8, 128), buf(4, 8, 128),
+        buf(4, 192, 128), buf(2, 192, 128), buf(192, 128), buf(192, 128), buf(NC, 8, 128), buf(NC, 8, 128), buf(4, 8, 128), buf(4, 8, 128),
         buf16(4, 192, 128), buf(4, 8, 128), buf(8, 128), buf(NC, 8, 128),
         buf16(96, 1024), buf16(96, 1024), buf(96, 1024), buf(NZ, 8, 1024), buf(2, 4, 8, 1024), buf(2, 4, 8, 1024),
         buf16(NZ, 16, 1024), buf16(NZ, 16, 1024), buf(16, 128), buf(16, 128), buf(NZ, 8, 128), buf(NZ, 8, 128),
         buf16(3, 128, 1024), buf16(3, 128, 1024),
-        *sems(3, 3, 2, 16, 16, 16, 16, 7, 7, 7, 7, 7, 7, 7, 7),
+        *sems(3, 3, 2, 16, 16, 16, 16, 7, 7, 7, 7, 7, 7, 7, 7, 7, 7),
         *sems(3, 3, 3, 3, 3, 3, 3, 3, 3, 3, 3, 3),
         *sems(15, 15, 15, 15, 16, 16, 3, 3, 2),
     ]

time: 85.9 us -> 87.3 us (1.016)
  the two profiles are of different devices: /device:TPU:56 before, /device:TPU:8 now
where the time goes in v5:
time: 87.3 us; the launch traced here: 86.9 us
  Pallas kernels  80 us (92%)
  local copies, waits for them, and re-layouts  6.32 us (7%)
    pallas_call x1, Pallas kernels, body(): pl.pallas_call(kernel, out_shape=(jax.ShapeDtypeStruct((1, 128), F32), ja...  80 us
    unnamed x14, local copies, waits for them, and re-layouts  6.32 us

profile of v5, /device:TPU:8, one launch (start us, length us, event | category | flops | bytes accessed | tf_op | source)
XLA Modules:
  0.0 86.9 jit_solution(11802731530518790641)
XLA Ops:
  0.6 0.0 copy-start.4
  0.6 0.6 copy-done.4
  1.3 0.0 copy-start
  1.3 0.9 %copy-done = bf16[128,1024]{1,0:T(8,128)(2,1)S(1)} copy-done((bf16[128,1024]{1,0:T(8,128)(2,1)S(1)}, bf16[128,1024]{1,0:T(8,128)(2,1)}, u32[]{:S(2)}) %copy-start) | copy-done | bytes 262168
  2.2 0.0 copy-start.1
  2.2 0.8 copy-done.1
  3.0 0.0 copy-start.2
  3.0 0.7 copy-done.2
  3.7 0.0 copy-start.3
  3.7 0.7 copy-done.3
  4.4 80.0 %shard_map.84 = (f32[1,128]{1,0:T(1,128)S(1)}, f32[128,1024]{1,0:T(8,128)S(1)}, f32[6,1024]{1,0:T(8,128)S(1)}, f32[16,1024]{1,0:T(8,128)S(1)}) custom-call(bf16[128,1024]{1,0:T(8,128)(2,1)S(1)} %copy-done, bf16[6,1024]{1,0:T(8,128)(2,1)S(1)} %copy-done.2, bf16[16,1024]{1,0:T(8,128)(2,1)S(1)} %copy-done.1, s32[16,128]{1,0:T(8,128)S(1)} %bitcast.3, ...), custom_call_target="tpu_custom_call" | custom-call | tf_op jit(solution)/shard_map/pallas_call | solution.py:485
  84.4 0.5 copy.13
  84.9 0.8 copy.14
  85.7 0.6 copy.15
  86.3 0.6 copy.16
Async XLA Ops:
  0.6 0.7 copy-start.4
  1.3 0.9 %copy-start = (bf16[128,1024]{1,0:T(8,128)(2,1)S(1)}, bf16[128,1024]{1,0:T(8,128)(2,1)}, u32[]{:S(2)}) copy-start(bf16[128,1024]{1,0:T(8,128)(2,1)} %q_ref.1) | copy-start | bytes 786436
  2.2 0.8 copy-start.1
  3.0 0.7 copy-start.2
  3.7 0.7 copy-start.3
